TPU v7x, 32 devices: a whole 2x2x4 slice. The times are simulated.
32 devices in a mesh: batch: 16 (over z, y, core), span: 2 (over x).
Axes of the slice: x: 2, y: 2, z: 4, core: 2. Of those that a mesh axis runs over, the one named last changes fastest.
Arguments:
- image_tokens: bfloat16 [32, 256, 512], P('batch'), may hold values from -400 to 400
- captions: bfloat16 [256, 512], P(('batch', 'span')), may hold values from -6 to 6
- owner: int32 [256], P(('batch', 'span')), may hold values from 0 to 31
- w_query: bfloat16 [512, 512], replicated, may hold values from -0.25 to 0.25
- w_key: bfloat16 [512, 512], replicated, may hold values from -0.25 to 0.25
- w_value: bfloat16 [512, 512], replicated, may hold values from -0.25 to 0.25
- w_out: bfloat16 [512, 512], replicated, may hold values from -0.25 to 0.25
Outputs:
- caption_grad: float32 [256, 512], P(('batch', 'span'))
- token_grad: float32 [32, 256, 512], P('batch')
Inputs may be any that keep to these rules, and one draw needn't show every extreme that they name: `owner`: each caption names one image.
All inputs are finite; a program needn't handle non-finite values.
Results may differ from a plain program's by a relative error of at most 0.039.
The roundings to bfloat16 on the way count: a program that leaves them out, or rounds other values in their place, can miss the bound.
Values may be sent and summed in bfloat16 or wider, within the bound.
A program may use at most 64 MiB of HBM per device.

v0:
```python
import math

import jax
import jax.numpy as jnp
from jax import lax
from jax.sharding import PartitionSpec as P

HEADS = 8
HEAD_DIM = 64
D = 512


LOGIT_SCALE = 10.0
LOGIT_BIAS = -2.0
NORM_EPS = 1e-06


def pair_loss(query, keys, values, caption_f, w_out, owner_block, image_base):
    count = query.shape[0]
    images = keys.shape[0]
    patches = keys.shape[1]
    width = keys.shape[2]
    query_heads = query.reshape(count, HEADS, HEAD_DIM)
    key_heads = keys.reshape(images, patches, HEADS, HEAD_DIM)
    value_heads = values.reshape(images, patches, HEADS, HEAD_DIM)
    scores = jnp.einsum(
        "che,iphe->cihp", query_heads, key_heads, preferred_element_type=jnp.float32
    ) * HEAD_DIM ** (-0.5)
    weights = jax.nn.softmax(scores, axis=-1).astype(jnp.bfloat16)
    pooled = jnp.einsum("cihp,iphe->cihe", weights, value_heads, preferred_element_type=jnp.float32)
    pooled = pooled.reshape(count * images, width).astype(jnp.bfloat16)
    mixed = jnp.dot(pooled, w_out, preferred_element_type=jnp.float32).reshape(count, images, width)
    inner = jnp.sum(mixed * caption_f[:, None, :], axis=-1)
    mixed_norm = jnp.sqrt(jnp.sum(mixed * mixed, axis=-1) + NORM_EPS)
    caption_norm = jnp.sqrt(jnp.sum(caption_f * caption_f, axis=-1) + NORM_EPS)
    cosine = inner / (mixed_norm * caption_norm[:, None])
    logits = LOGIT_SCALE * cosine + LOGIT_BIAS
    image_ids = image_base + jnp.arange(images, dtype=jnp.int32)
    labels = jnp.where(owner_block[:, None] == image_ids[None, :], 1.0, -1.0).astype(jnp.float32)
    return jnp.sum(jax.nn.softplus(-labels * logits))


def process(captions_in, owners_in, keys, values, w_query, w_out, image_base):
    rows = captions_in.shape[0]
    group = math.gcd(rows, 64)
    count = rows // group

    def step(carry, item):
        grad_keys, grad_values = carry
        caption_block, owner_block = item
        query = jnp.dot(caption_block, w_query, preferred_element_type=jnp.float32).astype(
            jnp.bfloat16
        )
        caption_f = caption_block.astype(jnp.float32)

        def local(query_in, keys_in, values_in, caption_in):
            return pair_loss(
                query_in, keys_in, values_in, caption_in, w_out, owner_block, image_base
            )

        value, pull = jax.vjp(local, query, keys, values, caption_f)
        grad_query, more_keys, more_values, grad_direct = pull(jnp.ones((), jnp.float32))
        grads = (grad_direct + jnp.dot(grad_query, w_query.T, preferred_element_type=jnp.float32))[
            None
        ]
        carry = (
            grad_keys + more_keys.astype(jnp.float32),
            grad_values + more_values.astype(jnp.float32),
        )
        return (carry, grads)

    init = (jnp.zeros(keys.shape, jnp.float32), jnp.zeros(values.shape, jnp.float32))
    items = (captions_in.reshape(count, group, D), owners_in.reshape(count, group))
    (grad_keys, grad_values), grads = lax.scan(step, init, items)
    layers = grads.shape[1]
    grads = jnp.transpose(grads, (1, 0, 2, 3)).reshape(layers, rows, D)
    return (grad_keys, grad_values, grads)


def on_device(image_tokens, captions, owner, w_query, w_key, w_value, w_out):
    images = image_tokens.shape[0]
    patches = image_tokens.shape[1]
    token_rows = image_tokens.reshape(images * patches, D)
    keys = (
        jnp.dot(token_rows, w_key, preferred_element_type=jnp.float32)
        .astype(jnp.bfloat16)
        .reshape(images, patches, D)
    )
    values = (
        jnp.dot(token_rows, w_value, preferred_element_type=jnp.float32)
        .astype(jnp.bfloat16)
        .reshape(images, patches, D)
    )
    image_base = lax.axis_index("batch") * images
    more_keys, more_values, grads = process(
        lax.all_gather(captions, "batch", axis=0, tiled=True),
        lax.all_gather(owner, "batch", axis=0, tiled=True),
        keys,
        values,
        w_query,
        w_out,
        image_base,
    )
    buffer = grads
    grad_keys, grad_values, buffer = (more_keys, more_values, buffer)
    summed = lax.psum_scatter(buffer, "batch", scatter_dimension=1, tiled=True)
    caption_grad = summed[0]
    caption_grad = 16.0 * caption_grad
    keys_b = grad_keys.reshape(images * patches, D).astype(jnp.bfloat16)
    values_b = grad_values.reshape(images * patches, D).astype(jnp.bfloat16)
    token_part = jnp.dot(keys_b, w_key.T, preferred_element_type=jnp.float32)
    token_part = token_part + jnp.dot(values_b, w_value.T, preferred_element_type=jnp.float32)
    token_grad = lax.psum(patches * token_part, "span").reshape(images, patches, D)
    return (caption_grad, token_grad)


def solution(mesh):
    placed = (
        P("batch", None, None),
        P(("batch", "span"), None),
        P(("batch", "span")),
        P(),
        P(),
        P(),
        P(),
    )
    return jax.shard_map(
        on_device,
        mesh=mesh,
        in_specs=placed,
        out_specs=(P(("batch", "span"), None), P("batch", None, None)),
        check_vma=False,
    )
```

profile of v0, /device:TPU:0, one launch (start us, length us, event | category | flops | bytes accessed | tf_op | source)
XLA Modules:
  0.0 149.6 jit_solution(10582914579873162241)
XLA Ops:
  9.0 1.5 convolution_convert_fusion.7
  15.9 13.7 %all-reduce = s32[128]{0:T(128)S(1)} all-reduce(s32[128]{0:T(128)S(1)} %dynamic-update-slice), channel_id=1, replica_groups=mesh['batch'=16,'span'=2] {'batch'}, use_global_device_ids=true, to_apply=%add | all-reduce | flops 128 | bytes 1024
  29.7 18.3 %all_gather.6 = bf16[128,512]{1,0:T(8,128)(2,1)S(1)} all-gather(bf16[8,512]{1,0:T(8,128)(2,1)S(1)} %copy-done.8), channel_id=1, replica_groups=mesh['batch'=16,'span'=2] {'batch'}, dimensions={0}, use_global_device_ids=true | all-gather | bytes 139264 | tf_op jit(solution)/shard_map/all_gather | solution.py:96
  48.0 37.3 %while.16 = (s32[]{:T(128)}, f32[2,256,512]{1,2,0:T(8,128)}, f32[2,256,512]{1,2,0:T(8,128)}, f32[2,1,64,512]{3,2,1,0:T(8,128)}, bf16[2,64,512]{2,1,0:T(8,128)(2,...) while((s32[]{:T(128)}, f32[2,256,512]{1,2,0:T(8,128)}, ...), condition=%wide.wide.region_9.10_spmd.clone, body=%wide.wide.region_0.9_spmd.clone.sunk | while | flops 412422400 | bytes 35671052 | solution.py:74
  49.6 1.5 bitcast_reduce_fusion.3
  53.2 1.4 multiply_reduce_fusion.13
  55.2 1.3 fusion.131
  56.8 1.6 %fusion.133 = (f32[64,2,8]{0,1,2:T(2,128)S(1)}, bf16[2,8,64,256]{3,2,0,1:T(8,128)(2,1)S(1)}) fusion(f32[8,64,2,256]{3,1,2,0:T(8,128)S(1)} %get-tuple-element.308, f32[64,2,8]{0,1,2:T(2,128)S(1)} %multiply_divide_fusion.4, f32[64,2,8]{0,1,2:T(2,128)S(1)} %get-tuple-element.309, bf16[2,256,8,64]{1,0,3,2:T(2,128)(2,1)} %get-tuple-element.364, ...), kind=kOutput, calls=%fused_computation.25.clone.clone.1 | convolution fusion | flops 35126272 | bytes 2240512 | tf_op jit(solution)/shard_map/while/body/eval_jaxpr/transpose(jvp(cihp,iphe->cihe))/dot_general | solution.py:30
  58.4 1.8 %fusion.135 = bf16[64,8,64]{2,0,1:T(8,128)(2,1)S(1)} fusion(bf16[2,256,8,64]{1,0,3,2:T(2,128)(2,1)} %get-tuple-element.363, bf16[2,8,64,256]{3,2,0,1:T(8,128)(2,1)S(1)} %get-tuple-element.317, f32[8,64,2,256]{3,1,2,0:T(8,128)S(1)} %get-tuple-element.308, f32[8,2,64]{2,1,0:T(2,128)S(1)} %bitcast.233, f32[8,2,64]{2,1,0:T(2,128)S(1)} %negate_bitcast_fusion.3, ...), kind=kOutput, calls=%fused_computation.17.clone.clone.1 | convolution fusion | flops 35160064 | bytes 2174976 | tf_op jit(solution)/shard_map/while/body/eval_jaxpr/transpose(jvp(che,iphe->cihp))/dot_general | solution.py:26
  60.6 2.0 %fusion.136 = f32[2,1,64,512]{3,2,1,0:T(8,128)} fusion(f32[2,1,64,512]{3,2,1,0:T(8,128)} %get-tuple-element.340, s32[]{:T(128)} %get-tuple-element.337, bf16[64,512]{1,0:T(8,128)(2,1)S(1)} %reshape.111, bf16[512,512]{1,0:T(8,128)(2,1)} %get-tuple-element.357, f32[64,512]{1,0:T(8,128)S(1)} %multiply_reduce_fusion.16, ...), kind=kOutput, calls=%fused_computation.16.clone.clone.1 | convolution fusion | flops 33718272 | bytes 918272 | tf_op jit(solution)/shard_map/while/body/eval_jaxpr/dot_general | solution.py:63
  64.2 1.7 %bitcast_add_fusion.4 = (f32[2,256,512]{1,2,0:T(8,128)}, f32[2,256,512]{1,2,0:T(8,128)}) fusion(f32[2,8,64,256]{3,2,1,0:T(8,128)S(1)} %fusion.132, f32[2,256,512]{1,2,0:T(8,128)} %get-tuple-element.339, pred[]{:T(512)S(6)} %compare.4, f32[2,256,8,64]{1,3,2,0:T(8,128)S(1)} %copy.127, f32[2,256,512]{1,2,0:T(8,128)} %get-tuple-element.338), kind=kLoop, calls=%fused_computation.26.clone.clone.1 | loop fusion | flops 1048576 | bytes 6291457 | tf_op jit(solution)/shard_map/while/body/eval_jaxpr/add | solution.py:68
  67.5 1.5 bitcast_reduce_fusion.3
  71.1 1.4 multiply_reduce_fusion.13
  73.1 1.3 fusion.131
  74.7 1.6 %fusion.133 = (f32[64,2,8]{0,1,2:T(2,128)S(1)}, bf16[2,8,64,256]{3,2,0,1:T(8,128)(2,1)S(1)}) fusion(f32[8,64,2,256]{3,1,2,0:T(8,128)S(1)} %get-tuple-element.308, f32[64,2,8]{0,1,2:T(2,128)S(1)} %multiply_divide_fusion.4, f32[64,2,8]{0,1,2:T(2,128)S(1)} %get-tuple-element.309, bf16[2,256,8,64]{1,0,3,2:T(2,128)(2,1)} %get-tuple-element.364, ...), kind=kOutput, calls=%fused_computation.25.clone.clone.1 | convolution fusion | flops 35126272 | bytes 2240512 | tf_op jit(solution)/shard_map/while/body/eval_jaxpr/transpose(jvp(cihp,iphe->cihe))/dot_general | solution.py:30
  76.3 1.8 %fusion.135 = bf16[64,8,64]{2,0,1:T(8,128)(2,1)S(1)} fusion(bf16[2,256,8,64]{1,0,3,2:T(2,128)(2,1)} %get-tuple-element.363, bf16[2,8,64,256]{3,2,0,1:T(8,128)(2,1)S(1)} %get-tuple-element.317, f32[8,64,2,256]{3,1,2,0:T(8,128)S(1)} %get-tuple-element.308, f32[8,2,64]{2,1,0:T(2,128)S(1)} %bitcast.233, f32[8,2,64]{2,1,0:T(2,128)S(1)} %negate_bitcast_fusion.3, ...), kind=kOutput, calls=%fused_computation.17.clone.clone.1 | convolution fusion | flops 35160064 | bytes 2174976 | tf_op jit(solution)/shard_map/while/body/eval_jaxpr/transpose(jvp(che,iphe->cihp))/dot_general | solution.py:26
  78.5 2.0 %fusion.136 = f32[2,1,64,512]{3,2,1,0:T(8,128)} fusion(f32[2,1,64,512]{3,2,1,0:T(8,128)} %get-tuple-element.340, s32[]{:T(128)} %get-tuple-element.337, bf16[64,512]{1,0:T(8,128)(2,1)S(1)} %reshape.111, bf16[512,512]{1,0:T(8,128)(2,1)} %get-tuple-element.357, f32[64,512]{1,0:T(8,128)S(1)} %multiply_reduce_fusion.16, ...), kind=kOutput, calls=%fused_computation.16.clone.clone.1 | convolution fusion | flops 33718272 | bytes 918272 | tf_op jit(solution)/shard_map/while/body/eval_jaxpr/dot_general | solution.py:63
  82.1 3.2 %bitcast_add_fusion.4 = (f32[2,256,512]{1,2,0:T(8,128)}, f32[2,256,512]{1,2,0:T(8,128)}) fusion(f32[2,8,64,256]{3,2,1,0:T(8,128)S(1)} %fusion.132, f32[2,256,512]{1,2,0:T(8,128)} %get-tuple-element.339, pred[]{:T(512)S(6)} %compare.4, f32[2,256,8,64]{1,3,2,0:T(8,128)S(1)} %copy.127, f32[2,256,512]{1,2,0:T(8,128)} %get-tuple-element.338), kind=kLoop, calls=%fused_computation.26.clone.clone.1 | loop fusion | flops 1048576 | bytes 6291457 | tf_op jit(solution)/shard_map/while/body/eval_jaxpr/add | solution.py:68
  85.4 2.3 %copy.55 = bf16[2,256,512]{2,1,0:T(8,128)(2,1)} copy(f32[2,256,512]{1,2,0:T(8,128)} %get-tuple-element.62) | data formatting | bytes 1572864 | tf_op jit(solution)/shard_map/while | solution.py:74
  87.7 1.6 %fusion.45 = f32[512,512]{1,0:T(8,128)S(1)} fusion(bf16[512,512]{1,0:T(8,128)(2,1)} %bitcast.232, bf16[512,512]{1,0:T(8,128)(2,1)S(1)} %copy-done.2), kind=kOutput, calls=%fused_computation.84 | convolution fusion | flops 268435456 | bytes 2097152 | tf_op jit(solution)/shard_map/dot_general | solution.py:111
  90.4 2.5 %fusion.41 = f32[512,512]{1,0:T(8,128)} fusion(f32[512,512]{1,0:T(8,128)S(1)} %fusion.45, bf16[512,512]{1,0:T(8,128)(2,1)} %bitcast.231, bf16[512,512]{1,0:T(8,128)(2,1)S(1)} %copy-done.4), kind=kOutput, calls=%fused_computation.79 | convolution fusion | flops 268959744 | bytes 3145728 | tf_op jit(solution)/shard_map/dot_general | solution.py:112
  92.9 45.7 %reduce-scatter.2.cloned.1.call-done = f32[1,8,512]{2,1,0:T(8,128)} async-done(((f32[1,128,512]{2,1,0:T(8,128)}), f32[1,8,512]{2,1,0:T(8,128)}) %reduce-scatter.2.cloned.1.call-update) | async-done | bytes 16400 | tf_op jit(solution)/shard_map/reduce_scatter | solution.py:106
  138.6 1.3 multiply_bitcast_fusion
  139.9 2.3 %copy.144 = f32[2,256,512]{2,1,0:T(8,128)} copy(f32[2,256,512]{2,1,0:T(8,128)} %all-reduce.3.cloned.1.call-done) | data formatting | bytes 2097152
  (108 shorter events, 19.6 us)
Async XLA Ops:
  8.0 1.0 copy-start
  8.0 130.6 %reduce-scatter.2.cloned.1.call-start = ((), (), s32[]{:S(2)}) async-start(), calls=%async_computation.1 | async-start | bytes 278528 | tf_op jit(solution)/shard_map/reduce_scatter | solution.py:106
  10.7 1.0 copy-start.5
  10.7 1.4 copy-start.3
  12.8 1.1 copy-start.6
  12.8 2.8 %copy-start.9 = (s32[8]{0:T(128)S(1)}, s32[8]{0:T(128)}, u32[]{:S(2)}) copy-start(s32[8]{0:T(128)} %param.11) | copy-start | bytes 100
  13.9 0.7 copy-start.10
  15.6 14.1 %copy-start.8 = (bf16[8,512]{1,0:T(8,128)(2,1)S(1)}, bf16[8,512]{1,0:T(8,128)(2,1)}, u32[]{:S(2)}) copy-start(bf16[8,512]{1,0:T(8,128)(2,1)} %param.10) | copy-start | bytes 24580
  51.5 1.0 copy-start.7
  58.4 1.9 %copy-start.11 = (bf16[2,8,64,256]{3,2,0,1:T(8,128)(2,1)}, bf16[2,8,64,256]{3,2,0,1:T(8,128)(2,1)S(1)}, u32[]{:S(2)}) copy-start(bf16[2,8,64,256]{3,2,0,1:T(8,128)(2,1)S(1)} %get-tuple-element.317) | copy-start | bytes 1572868 | tf_op jit(solution)/shard_map/while
  60.6 2.0 %copy-start.12 = (bf16[2,8,64,256]{3,2,0,1:T(8,128)(2,1)S(1)}, bf16[2,8,64,256]{3,2,0,1:T(8,128)(2,1)}, u32[]{:S(2)}) copy-start(bf16[2,8,64,256]{3,2,0,1:T(8,128)(2,1)} %copy-done.11) | copy-start | bytes 1572868 | tf_op jit(solution)/shard_map/while
  69.4 1.0 copy-start.7
  76.3 1.9 %copy-start.11 = (bf16[2,8,64,256]{3,2,0,1:T(8,128)(2,1)}, bf16[2,8,64,256]{3,2,0,1:T(8,128)(2,1)S(1)}, u32[]{:S(2)}) copy-start(bf16[2,8,64,256]{3,2,0,1:T(8,128)(2,1)S(1)} %get-tuple-element.317) | copy-start | bytes 1572868 | tf_op jit(solution)/shard_map/while
  78.5 2.1 %copy-start.12 = (bf16[2,8,64,256]{3,2,0,1:T(8,128)(2,1)S(1)}, bf16[2,8,64,256]{3,2,0,1:T(8,128)(2,1)}, u32[]{:S(2)}) copy-start(bf16[2,8,64,256]{3,2,0,1:T(8,128)(2,1)} %copy-done.11) | copy-start | bytes 1572868 | tf_op jit(solution)/shard_map/while
  85.3 54.6 %all-reduce.3.cloned.1.call-start = ((), (), s32[]{:S(2)}) async-start(), calls=%async_computation.2 | async-start | bytes 2097152 | tf_op jit(solution)/shard_map/psum | solution.py:113
  85.4 2.3 %copy-start.2 = (bf16[512,512]{1,0:T(8,128)(2,1)S(1)}, bf16[512,512]{1,0:T(8,128)(2,1)}, u32[]{:S(2)}) copy-start(bf16[512,512]{1,0:T(8,128)(2,1)} %param.13) | copy-start | bytes 1572868
  87.7 1.6 %copy-start.1 = (f32[2,256,512]{1,2,0:T(8,128)S(1)}, f32[2,256,512]{1,2,0:T(8,128)}, u32[]{:S(2)}) copy-start(f32[2,256,512]{1,2,0:T(8,128)} %get-tuple-element.63) | copy-start | bytes 3145732
  89.3 1.1 copy-start.4
Sparse Core Ops, SparseCore 0:
  85.5 53.1 reduce-scatter.1
Sparse Core Ops, SparseCore 1:
  93.0 37.7 all-reduce.2
where the time goes:
time: 151 us; the launch traced here: 150 us
  waiting for transfers between devices  45.8 us (30%)
  blocking collectives  32 us (21%)
  matrix products  30.7 us (20%)
  between operations  16.2 us (11%)
  local copies, waits for them, and re-layouts  15.7 us (10%)
  other arithmetic  8.75 us (6%)
    reduce_scatter x1, waiting for transfers between devices, on_device(): summed = lax.psum_scatter(buffer, 'batch', scatter_dimension=1, tiled=True)  45.7 us
    all_gather x1, blocking collectives, on_device(): lax.all_gather(captions, 'batch', axis=0, tiled=True)  18.3 us
    unnamed x1, blocking collectives  13.7 us
    dot_general x6, matrix products, pair_loss(): jnp.einsum('che,iphe->cihp', query_heads, key_heads, preferred_element_ty...  8.41 us
    unnamed x26, local copies, waits for them, and re-layouts  5.66 us
    dot_general x4, matrix products, pair_loss(): jnp.dot(pooled, w_out, preferred_element_type=jnp.float32)  5.44 us
    add x2, other arithmetic, step(): grad_values + more_values.astype(jnp.float32)  4.91 us
    dot_general x6, matrix products, pair_loss(): jnp.einsum('cihp,iphe->cihe', weights, value_heads, preferred_element_typ...  4.34 us
  transfers between devices with their start and end apart: 2, of which 1 were waited for; matrix products, arithmetic and copies ran while one was open for 6% of the time, Pallas kernels for 0%

commit v1 on v0

v1 whole, which is shorter than its diff:
```python
import functools
import math

import jax
import jax.numpy as jnp
from jax import lax
from jax.experimental import pallas as pl
from jax.experimental.pallas import tpu as pltpu
from jax.sharding import PartitionSpec as P

HEAD_DIM = 64
LOGIT_SCALE = 10.0
LOGIT_BIAS = -2.0
NORM_EPS = 1e-06
CAPTION_SCALE = 16.0
LANES = 128
GROUP = 256
HEADS_IN_GROUP = GROUP // HEAD_DIM
F32 = jnp.float32
BF16 = jnp.bfloat16
MESH = pl.DeviceIdType.MESH


def dot(a, b):
    return jnp.dot(a, b, preferred_element_type=F32)


def dot_t(a, b):
    return lax.dot_general(a, b, (((1,), (1,)), ((), ())), preferred_element_type=F32)


def head_stack(x):
    head = lax.broadcasted_iota(jnp.int32, x.shape, 1) // HEAD_DIM
    return jnp.concatenate(
        [jnp.where(head == h, x, jnp.zeros_like(x)) for h in range(HEADS_IN_GROUP)], axis=0
    )


def head_blocks(x, width):
    return jnp.concatenate(
        [
            x[h * HEAD_DIM : (h + 1) * HEAD_DIM, h * width : (h + 1) * width]
            for h in range(HEADS_IN_GROUP)
        ],
        axis=0,
    )


def pair_kernel(
    nb,
    ns,
    images,
    captions_ref,
    owner_ref,
    tokens_hbm,
    wq_hbm,
    wk_hbm,
    wv_hbm,
    wo_hbm,
    gk_out,
    gv_out,
    sum_out,
    tokens,
    wq,
    wk,
    wv,
    wo,
    keys,
    values,
    keys_t,
    values_t,
    prob,
    prob_b,
    gk,
    gv,
    caps,
    part,
    parts_in,
    load_sem,
    cap_send,
    cap_recv,
    span_send,
    span_recv,
    part_send,
    part_recv,
):
    me = lax.axis_index("batch")
    my_span = lax.axis_index("span")
    rows = captions_ref.shape[0]
    d = captions_ref.shape[1]
    half = d // 2
    patches = tokens.shape[0] // images
    groups = d // GROUP
    block = math.gcd(nb * rows, LANES)
    slots = block // rows
    blocks = nb * rows // block
    stacked = HEADS_IN_GROUP * block

    def peer_of(step):
        return lax.rem(me + step, nb)

    def span_of(step):
        return lax.rem(my_span + step, ns)

    barrier = pltpu.get_barrier_semaphore()

    @pl.loop(1, nb)
    def _(step):
        pl.semaphore_signal(
            barrier, inc=1, device_id={"batch": peer_of(step)}, device_id_type=MESH
        )

    for step in range(1, ns):
        pl.semaphore_signal(
            barrier, inc=1, device_id={"span": span_of(step)}, device_id_type=MESH
        )

    loads = [
        pltpu.make_async_copy(src, dst, load_sem.at[n])
        for n, (src, dst) in enumerate(
            ((tokens_hbm, tokens), (wk_hbm, wk), (wv_hbm, wv), (wq_hbm, wq), (wo_hbm, wo))
        )
    ]
    for load in loads:
        load.start()

    mine = captions_ref[...].astype(F32)
    folded = jnp.concatenate([mine[:, :half], mine[:, half:]], axis=0)
    owners = jnp.broadcast_to(owner_ref[...].astype(F32), (rows, LANES))
    owners = jnp.concatenate([owners, owners], axis=0)
    caps[0, me] = jnp.concatenate([folded, owners], axis=1).astype(BF16)

    pl.semaphore_wait(barrier, nb + ns - 2)

    def cap_copy(step, slot):
        return pltpu.make_async_remote_copy(
            src_ref=caps.at[0, me],
            dst_ref=caps.at[0, me],
            send_sem=cap_send.at[step],
            recv_sem=cap_recv.at[slot],
            device_id={"batch": peer_of(step)},
            device_id_type=MESH,
        )

    def part_copy(step, slot):
        return pltpu.make_async_remote_copy(
            src_ref=part.at[peer_of(step)],
            dst_ref=parts_in.at[me],
            send_sem=part_send.at[step],
            recv_sem=part_recv.at[slot],
            device_id={"batch": peer_of(step)},
            device_id_type=MESH,
        )

    def span_copy(step, slot):
        return pltpu.make_async_remote_copy(
            src_ref=caps.at[0],
            dst_ref=caps.at[ns - step],
            send_sem=span_send.at[step],
            recv_sem=span_recv.at[slot],
            device_id={"span": span_of(step)},
            device_id_type=MESH,
        )

    @pl.loop(1, nb)
    def _(step):
        cap_copy(step, me).start()

    for load in loads[:3]:
        load.wait()
    for i in range(images):
        at = pl.ds(i * patches, patches)
        found = dot(tokens[at, :], wk[...])
        keys[at, :] = found.astype(BF16)
        keys_t[:, at] = found.T.astype(BF16)
        found = dot(tokens[at, :], wv[...])
        values[at, :] = found.astype(BF16)
        values_t[:, at] = found.T.astype(BF16)
    gk[...] = jnp.zeros_like(gk)
    gv[...] = jnp.zeros_like(gv)
    for load in loads[3:]:
        load.wait()

    @pl.loop(1, nb)
    def _(step):
        cap_copy(step, peer_of(step)).wait_recv()

    for step in range(1, ns):
        span_copy(step, ns - step).start()

    def run_block(slot, which, own):
        held = caps[which, pl.ds(slot, slots)].astype(F32)
        caption = jnp.concatenate(
            [
                held[:, :rows, :half].reshape(block, half),
                held[:, rows:, :half].reshape(block, half),
            ],
            axis=1,
        )
        owner = held[:, :rows, half:].reshape(block, LANES)[:, :1]
        query = (dot(caption.astype(BF16), wq[...]) * HEAD_DIM**-0.5).astype(BF16)
        queries = [head_stack(query[:, g * GROUP : (g + 1) * GROUP]) for g in range(groups)]

        pooled = []
        for i in range(images):
            at = slice(i * patches, (i + 1) * patches)
            found = []
            for g in range(groups):
                cols = slice(g * GROUP, (g + 1) * GROUP)
                to = slice(g * stacked, (g + 1) * stacked)
                scores = dot_t(keys[at, cols], queries[g])
                scores = jnp.exp(scores - jnp.max(scores, axis=0, keepdims=True))
                scores = scores * (1.0 / jnp.sum(scores, axis=0, keepdims=True))
                prob[at, to] = scores
                weights = scores.astype(BF16)
                prob_b[at, to] = weights
                found.append(head_blocks(dot(values_t[cols, at], weights), block))
            pooled.append(jnp.concatenate(found, axis=0).T.astype(BF16))
        mixed = dot(jnp.concatenate(pooled, axis=0), wo[...])
        caption_2 = jnp.concatenate([caption] * images, axis=0)
        owner_2 = jnp.concatenate([owner] * images, axis=0)
        image = (
            lax.broadcasted_iota(jnp.int32, (images * block, 1), 0) // block + me * images
        ).astype(F32)
        inner = jnp.sum(mixed * caption_2, axis=1, keepdims=True)
        mixed_inv = lax.rsqrt(jnp.sum(mixed * mixed, axis=1, keepdims=True) + NORM_EPS)
        caption_inv = lax.rsqrt(jnp.sum(caption * caption, axis=1, keepdims=True) + NORM_EPS)
        caption_inv = jnp.concatenate([caption_inv] * images, axis=0)
        cosine = inner * mixed_inv * caption_inv
        logit = LOGIT_SCALE * cosine + LOGIT_BIAS
        label = jnp.where(owner_2 == image, 1.0, -1.0)
        slope = -LOGIT_SCALE * label / (1.0 + jnp.exp(label * logit))
        across = slope * mixed_inv * caption_inv
        grad_mixed = across * caption_2 - (slope * cosine * mixed_inv * mixed_inv) * mixed
        grad_pooled = dot_t(grad_mixed.astype(BF16), wo[...]).astype(BF16)
        if own:
            direct = across * mixed - (slope * cosine * caption_inv * caption_inv) * caption_2
            direct = sum(direct[i * block : (i + 1) * block] for i in range(images))

        grad_query = []
        for g in range(groups):
            cols = slice(g * GROUP, (g + 1) * GROUP)
            to = slice(g * stacked, (g + 1) * stacked)
            total = None
            for i in range(images):
                at = slice(i * patches, (i + 1) * patches)
                grads = head_stack(grad_pooled[i * block : (i + 1) * block, cols])
                grad_weights = dot_t(values[at, cols], grads)
                gv[at, cols] += dot(prob_b[at, to], grads)
                weights = prob[at, to]
                grad_scores = weights * (
                    grad_weights - jnp.sum(weights * grad_weights, axis=0, keepdims=True)
                )
                grad_scores = grad_scores.astype(BF16)
                gk[at, cols] += dot(grad_scores, queries[g])
                if own:
                    found = head_blocks(dot(keys_t[cols, at], grad_scores), block)
                    total = found if total is None else total + found
            grad_query.append(total)
        if own:
            grad_query = jnp.concatenate(grad_query, axis=0).T * HEAD_DIM**-0.5
            grad = direct + dot_t(grad_query.astype(BF16), wq[...])
            grad = grad.reshape(slots, rows, d)
            part[pl.ds(slot, slots)] = jnp.concatenate(
                [grad[:, :, :half], grad[:, :, half:]], axis=1
            ).astype(BF16)

    def run_all(which, own):
        if blocks == 1:
            run_block(0, which, own)
        else:

            @pl.loop(0, blocks)
            def _(n):
                run_block(n * slots, which, own)

    run_all(0, True)

    @pl.loop(1, nb)
    def _(step):
        part_copy(step, me).start()

    for step in range(1, ns):
        span_copy(step, step).wait_recv()
        run_all(step, False)

    gk_out[...] = gk[...].astype(BF16)
    gv_out[...] = gv[...].astype(BF16)

    @pl.loop(1, nb)
    def _(step):
        part_copy(step, peer_of(step)).wait_recv()

    parts_in[me] = part[me]
    sum_out[...] = jnp.sum(parts_in[...].astype(F32), axis=0)

    @pl.loop(1, nb)
    def _(step):
        cap_copy(step, me).wait_send()
        part_copy(step, me).wait_send()

    for step in range(1, ns):
        span_copy(step, ns - step).wait_send()


def token_kernel(patches, sum_ref, gk, gv, wk, wv, caption_out, token_out):
    rows, d = caption_out.shape
    summed = sum_ref[...] * CAPTION_SCALE
    caption_out[...] = jnp.concatenate([summed[:rows], summed[rows:]], axis=1)
    token_out[...] = patches * (dot_t(gk[...], wk[...]) + dot_t(gv[...], wv[...]))


def on_device(nb, ns, image_tokens, captions, owner, w_query, w_key, w_value, w_out):
    images, patches, d = image_tokens.shape
    rows = captions.shape[0]
    total = images * patches
    block = math.gcd(nb * rows, LANES)
    vmem = pl.BlockSpec(memory_space=pltpu.VMEM)
    anywhere = pl.BlockSpec(memory_space=pl.ANY)
    heads = d // HEAD_DIM
    dma = pltpu.SemaphoreType.DMA
    gk, gv, summed = pl.pallas_call(
        functools.partial(pair_kernel, nb, ns, images),
        out_shape=(
            jax.ShapeDtypeStruct((total, d), BF16),
            jax.ShapeDtypeStruct((total, d), BF16),
            jax.ShapeDtypeStruct((2 * rows, d // 2), F32),
        ),
        in_specs=[vmem, vmem] + [anywhere] * 5,
        out_specs=(vmem, vmem, vmem),
        scratch_shapes=[
            pltpu.VMEM((total, d), BF16),
            pltpu.VMEM((d, d), BF16),
            pltpu.VMEM((d, d), BF16),
            pltpu.VMEM((d, d), BF16),
            pltpu.VMEM((d, d), BF16),
            pltpu.VMEM((total, d), BF16),
            pltpu.VMEM((total, d), BF16),
            pltpu.VMEM((d, total), BF16),
            pltpu.VMEM((d, total), BF16),
            pltpu.VMEM((total, heads * block), F32),
            pltpu.VMEM((total, heads * block), BF16),
            pltpu.VMEM((total, d), F32),
            pltpu.VMEM((total, d), F32),
            pltpu.VMEM((ns, nb, 2 * rows, d // 2 + LANES), BF16),
            pltpu.VMEM((nb, 2 * rows, d // 2), BF16),
            pltpu.VMEM((nb, 2 * rows, d // 2), BF16),
            dma((5,)),
            dma((nb,)),
            dma((nb,)),
            dma((ns,)),
            dma((ns,)),
            dma((nb,)),
            dma((nb,)),
        ],
        compiler_params=pltpu.CompilerParams(
            collective_id=0, has_side_effects=True, vmem_limit_bytes=36 * 2**20
        ),
        name="pairs",
    )(
        captions,
        owner.reshape(rows, 1),
        image_tokens.reshape(total, d),
        w_query,
        w_key,
        w_value,
        w_out,
    )
    caption_grad, token_grad = pl.pallas_call(
        functools.partial(token_kernel, patches),
        out_shape=(
            jax.ShapeDtypeStruct((rows, d), F32),
            jax.ShapeDtypeStruct((total, d), F32),
        ),
        in_specs=[vmem] * 5,
        out_specs=(vmem, vmem),
        compiler_params=pltpu.CompilerParams(vmem_limit_bytes=16 * 2**20),
        name="token_grad",
    )(summed, gk, gv, w_key, w_value)
    return (caption_grad, token_grad.reshape(images, patches, d))


def solution(mesh):
    placed = (
        P("batch", None, None),
        P(("batch", "span"), None),
        P(("batch", "span")),
        P(),
        P(),
        P(),
        P(),
    )
    return jax.shard_map(
        functools.partial(on_device, mesh.shape["batch"], mesh.shape["span"]),
        mesh=mesh,
        in_specs=placed,
        out_specs=(P(("batch", "span"), None), P("batch", None, None)),
        check_vma=False,
    )
```

time: 151 us -> 30.9 us (0.20)
  waiting for transfers between devices: 45.8 us -> 0 us
  blocking collectives: 32 us -> 0 us
  matrix products: 30.7 us -> 0 us
  Pallas kernels: 0 us -> 23.9 us
  between operations: 16.2 us -> 0.65 us
  local copies, waits for them, and re-layouts: 15.7 us -> 5.95 us
  other arithmetic: 8.75 us -> 0 us
    reduce_scatter x1 -> x0, waiting for transfers between devices: 45.7 us -> none  [on_device(): summed = lax.psum_scatter(buffer, 'batch', scatter_dimension=1, tiled=True)]
    dot_general x24 -> x0, matrix products: 30.7 us -> none  [the longest x6 8.41 us: pair_loss(): jnp.einsum('che,iphe->cihp', query_heads, key_heads, preferred_element_ty...]
    pallas_call x0 -> x2, Pallas kernels: none -> 23.9 us  [the longest x1 22.1 us: on_device(): pl.pallas_call(functools.partial(pair_kernel, nb, ns, images), out_shape=...]
    all_gather x1 -> x0, blocking collectives: 18.3 us -> none  [on_device(): lax.all_gather(captions, 'batch', axis=0, tiled=True)]
    unnamed x1 -> x0, blocking collectives: 13.7 us -> none
    add x4 -> x0, other arithmetic: 4.92 us -> none  [the longest x2 4.91 us: step(): grad_values + more_values.astype(jnp.float32)]
    while x14 -> x0, local copies, waits for them, and re-layouts: 4.69 us -> none  [the longest x2 3.3 us: process(): (grad_keys, grad_values), grads = lax.scan(step, init, items)]
    another operation x2 -> x0, local copies, waits for them, and re-layouts: 1.96 us -> none  [the longest x1 1.03 us: pair_loss(): value_heads = values.reshape(images, patches, HEADS, HEAD_DIM)]
  transfers between devices with their start and end apart: 2 -> 0, of which waited for: 1 -> 0; matrix products, arithmetic and copies ran while one was open for 6% -> 0% of each run, Pallas kernels for 0% -> 0%
where the time goes in v1:
time: 30.9 us; the launch traced here: 30.5 us
  Pallas kernels  23.9 us (77%)
  local copies, waits for them, and re-layouts  5.95 us (19%)
  between operations  0.65 us (2%)
    pallas_call x1, Pallas kernels, on_device(): pl.pallas_call(functools.partial(pair_kernel, nb, ns, images), out_shape=...  22.1 us
    unnamed x12, local copies, waits for them, and re-layouts  5.21 us
    pallas_call x1, Pallas kernels, on_device(): pl.pallas_call(functools.partial(token_kernel, patches), out_shape=(jax.S...  1.72 us
    reshape x1, local copies, waits for them, and re-layouts, on_device(): owner.reshape(rows, 1)  0.74 us

profile of v1, /device:TPU:0, one launch (start us, length us, event | category | flops | bytes accessed | tf_op | source)
XLA Modules:
  0.0 30.5 jit_solution(1158055065892142246)
XLA Ops:
  0.6 0.0 copy-start.5
  0.6 0.7 %copy.9.owner_ref = s32[8,1]{1,0:T(8,128)S(1)} copy(s32[8,1]{0,1:T(1,128)} %bitcast.4) | data formatting | bytes 64 | tf_op jit(solution)/shard_map/reshape | solution.py:362
  1.4 0.0 copy-done.5
  1.4 0.0 copy-start
  1.4 1.0 %copy-done = bf16[512,512]{1,0:T(8,128)(2,1)S(1)} copy-done((bf16[512,512]{1,0:T(8,128)(2,1)S(1)}, bf16[512,512]{1,0:T(8,128)(2,1)}, u32[]{:S(2)}) %copy-start) | copy-done | bytes 524312
  2.4 0.0 copy-start.1
  2.4 1.0 %copy-done.1 = bf16[512,512]{1,0:T(8,128)(2,1)S(1)} copy-done((bf16[512,512]{1,0:T(8,128)(2,1)S(1)}, bf16[512,512]{1,0:T(8,128)(2,1)}, u32[]{:S(2)}) %copy-start.1) | copy-done | bytes 524312
  3.5 0.0 copy-start.2
  3.5 1.0 %copy-done.2 = bf16[2,256,512]{2,1,0:T(8,128)(2,1)S(1)} copy-done((bf16[2,256,512]{2,1,0:T(8,128)(2,1)S(1)}, bf16[2,256,512]{2,1,0:T(8,128)(2,1)}, u32[]{:S(2)}) %copy-start.2) | copy-done | bytes 524312
  4.5 0.0 copy-start.3
  4.5 1.0 %copy-done.3 = bf16[512,512]{1,0:T(8,128)(2,1)S(1)} copy-done((bf16[512,512]{1,0:T(8,128)(2,1)S(1)}, bf16[512,512]{1,0:T(8,128)(2,1)}, u32[]{:S(2)}) %copy-start.3) | copy-done | bytes 524312
  5.5 0.0 copy-start.4
  5.5 1.0 %copy-done.4 = bf16[512,512]{1,0:T(8,128)(2,1)S(1)} copy-done((bf16[512,512]{1,0:T(8,128)(2,1)S(1)}, bf16[512,512]{1,0:T(8,128)(2,1)}, u32[]{:S(2)}) %copy-start.4) | copy-done | bytes 524312
  6.6 22.1 %pairs.1 = (bf16[512,512]{1,0:T(8,128)(2,1)S(1)}, bf16[512,512]{1,0:T(8,128)(2,1)S(1)}, f32[16,256]{1,0:T(8,128)S(1)}) custom-call(bf16[8,512]{1,0:T(8,128)(2,1)S(1)} %copy-done.5, s32[8,1]{1,0:T(8,128)S(1)} %copy.9.owner_ref, bf16[512,512]{1,0:T(8,128)(2,1)S(1)} %bitcast.3, bf16[512,512]{1,0:T(8,128)(2,1)S(1)} %copy-done.3, bf16[512,512]{1,0:T(8,128)(2,1)S(1)} %copy-done, ...), custom_call_target="tpu_custom_call" | custom-call | tf_op jit(solution)/shard_map/pairs/pallas_call | solution.py:322
  28.7 1.7 %token_grad.1 = (f32[8,512]{1,0:T(8,128)}, f32[512,512]{1,0:T(8,128)}) custom-call(f32[16,256]{1,0:T(8,128)S(1)} %get-tuple-element.7.sum_ref, bf16[512,512]{1,0:T(8,128)(2,1)S(1)} %get-tuple-element.8.gk, bf16[512,512]{1,0:T(8,128)(2,1)S(1)} %get-tuple-element.9.gv, bf16[512,512]{1,0:T(8,128)(2,1)S(1)} %copy-done, bf16[512,512]{1,0:T(8,128)(2,1)S(1)} %copy-done.1), custom_call_target="tpu_custom_call" | custom-call | tf_op jit(solution)/shard_map/token_grad/pallas_call | solution.py:369
Async XLA Ops:
  0.6 0.7 %copy-start.5 = (bf16[8,512]{1,0:T(8,128)(2,1)S(1)}, bf16[8,512]{1,0:T(8,128)(2,1)}, u32[]{:S(2)}) copy-start(bf16[8,512]{1,0:T(8,128)(2,1)} %captions_ref.1) | copy-start | bytes 24580
  1.4 1.0 %copy-start = (bf16[512,512]{1,0:T(8,128)(2,1)S(1)}, bf16[512,512]{1,0:T(8,128)(2,1)}, u32[]{:S(2)}) copy-start(bf16[512,512]{1,0:T(8,128)(2,1)} %wk.1) | copy-start | bytes 1572868
  2.4 1.0 %copy-start.1 = (bf16[512,512]{1,0:T(8,128)(2,1)S(1)}, bf16[512,512]{1,0:T(8,128)(2,1)}, u32[]{:S(2)}) copy-start(bf16[512,512]{1,0:T(8,128)(2,1)} %wv.1) | copy-start | bytes 1572868
  3.5 1.0 %copy-start.2 = (bf16[2,256,512]{2,1,0:T(8,128)(2,1)S(1)}, bf16[2,256,512]{2,1,0:T(8,128)(2,1)}, u32[]{:S(2)}) copy-start(bf16[2,256,512]{2,1,0:T(8,128)(2,1)} %param.7) | copy-start | bytes 1572868
  4.5 1.0 %copy-start.3 = (bf16[512,512]{1,0:T(8,128)(2,1)S(1)}, bf16[512,512]{1,0:T(8,128)(2,1)}, u32[]{:S(2)}) copy-start(bf16[512,512]{1,0:T(8,128)(2,1)} %wq_hbm.1) | copy-start | bytes 1572868
  5.5 1.0 %copy-start.4 = (bf16[512,512]{1,0:T(8,128)(2,1)S(1)}, bf16[512,512]{1,0:T(8,128)(2,1)}, u32[]{:S(2)}) copy-start(bf16[512,512]{1,0:T(8,128)(2,1)} %wo_hbm.1) | copy-start | bytes 1572868

commit v2 on v1

--- a/solution.py
+++ b/solution.py
@@ -46,12 +46,21 @@
     )
 
 
+def head_columns(parts, width):
+    parts = [
+        part[:, h * width : (h + 1) * width] for part in parts for h in range(HEADS_IN_GROUP)
+    ]
+    return jnp.concatenate(
+        [jnp.broadcast_to(part, (HEAD_DIM, width)) for part in parts], axis=0
+    ).T
+
+
 def pair_kernel(
     nb,
     ns,
     images,
-    captions_ref,
-    owner_ref,
+    captions_hbm,
+    owner_hbm,
     tokens_hbm,
     wq_hbm,
     wk_hbm,
@@ -60,27 +69,33 @@
     gk_out,
     gv_out,
     sum_out,
+    wk,
+    wv,
+    captions_ref,
+    owner_ref,
     tokens,
     wq,
-    wk,
-    wv,
     wo,
     keys,
     values,
     keys_t,
     values_t,
-    prob,
-    prob_b,
+    weights_ref,
     gk,
     gv,
     caps,
+    owners,
     part,
     parts_in,
     load_sem,
     cap_send,
     cap_recv,
+    owner_send,
+    owner_recv,
     span_send,
     span_recv,
+    span_owner_send,
+    span_owner_recv,
     part_send,
     part_recv,
 ):
@@ -102,6 +117,23 @@
     def span_of(step):
         return lax.rem(my_span + step, ns)
 
+    loads = [
+        pltpu.make_async_copy(src, dst, load_sem.at[n])
+        for n, (src, dst) in enumerate(
+            (
+                (captions_hbm, captions_ref),
+                (owner_hbm, owner_ref),
+                (tokens_hbm, tokens),
+                (wk_hbm, wk),
+                (wv_hbm, wv),
+                (wq_hbm, wq),
+                (wo_hbm, wo),
+            )
+        )
+    ]
+    for load in loads[:2]:
+        load.start()
+
     barrier = pltpu.get_barrier_semaphore()
 
     @pl.loop(1, nb)
@@ -115,20 +147,15 @@
             barrier, inc=1, device_id={"span": span_of(step)}, device_id_type=MESH
         )
 
-    loads = [
-        pltpu.make_async_copy(src, dst, load_sem.at[n])
-        for n, (src, dst) in enumerate(
-            ((tokens_hbm, tokens), (wk_hbm, wk), (wv_hbm, wv), (wq_hbm, wq), (wo_hbm, wo))
-        )
-    ]
-    for load in loads:
+    for load in loads[2:]:
         load.start()
-
+    for load in loads[:2]:
+        load.wait()
     mine = captions_ref[...].astype(F32)
-    folded = jnp.concatenate([mine[:, :half], mine[:, half:]], axis=0)
-    owners = jnp.broadcast_to(owner_ref[...].astype(F32), (rows, LANES))
-    owners = jnp.concatenate([owners, owners], axis=0)
-    caps[0, me] = jnp.concatenate([folded, owners], axis=1).astype(BF16)
+    caps[0, me] = jnp.concatenate([mine[:, :half], mine[:, half:]], axis=0).astype(BF16)
+    owners[0, me] = jnp.concatenate(
+        [owner_ref[...], jnp.zeros((1, LANES - rows), jnp.int32)], axis=1
+    )
 
     pl.semaphore_wait(barrier, nb + ns - 2)
 
@@ -142,6 +169,16 @@
             device_id_type=MESH,
         )
 
+    def owner_copy(step, slot):
+        return pltpu.make_async_remote_copy(
+            src_ref=owners.at[0, me],
+            dst_ref=owners.at[0, me],
+            send_sem=owner_send.at[step],
+            recv_sem=owner_recv.at[slot],
+            device_id={"batch": peer_of(step)},
+            device_id_type=MESH,
+        )
+
     def part_copy(step, slot):
         return pltpu.make_async_remote_copy(
             src_ref=part.at[peer_of(step)],
@@ -162,11 +199,25 @@
             device_id_type=MESH,
         )
 
+    def span_owner_copy(step, slot):
+        return pltpu.make_async_remote_copy(
+            src_ref=owners.at[0],
+            dst_ref=owners.at[ns - step],
+            send_sem=span_owner_send.at[step],
+            recv_sem=span_owner_recv.at[slot],
+            device_id={"span": span_of(step)},
+            device_id_type=MESH,
+        )
+
     @pl.loop(1, nb)
     def _(step):
         cap_copy(step, me).start()
 
-    for load in loads[:3]:
+    @pl.loop(1, nb)
+    def _(step):
+        owner_copy(step, me).start()
+
+    for load in loads[2:5]:
         load.wait()
     for i in range(images):
         at = pl.ds(i * patches, patches)
@@ -178,7 +229,7 @@
         values_t[:, at] = found.T.astype(BF16)
     gk[...] = jnp.zeros_like(gk)
     gv[...] = jnp.zeros_like(gv)
-    for load in loads[3:]:
+    for load in loads[5:]:
         load.wait()
 
     @pl.loop(1, nb)
@@ -187,34 +238,52 @@
 
     for step in range(1, ns):
         span_copy(step, ns - step).start()
+
+    @pl.loop(1, nb)
+    def _(step):
+        owner_copy(step, peer_of(step)).wait_recv()
+
+    for step in range(1, ns):
+        span_owner_copy(step, ns - step).start()
 
     def run_block(slot, which, own):
         held = caps[which, pl.ds(slot, slots)].astype(F32)
         caption = jnp.concatenate(
             [
-                held[:, :rows, :half].reshape(block, half),
-                held[:, rows:, :half].reshape(block, half),
+                held[:, :rows].reshape(block, half),
+                held[:, rows:].reshape(block, half),
             ],
             axis=1,
         )
-        owner = held[:, :rows, half:].reshape(block, LANES)[:, :1]
+        owner = owners[which, pl.ds(slot, slots)]
+        owner = jnp.broadcast_to(owner, (slots, rows, LANES))
+        row = lax.broadcasted_iota(jnp.int32, owner.shape, 1)
+        lane = lax.broadcasted_iota(jnp.int32, owner.shape, 2)
+        owner = jnp.sum(
+            jnp.where(row == lane, owner, 0).astype(F32).reshape(block, LANES),
+            axis=1,
+            keepdims=True,
+        )
         query = (dot(caption.astype(BF16), wq[...]) * HEAD_DIM**-0.5).astype(BF16)
         queries = [head_stack(query[:, g * GROUP : (g + 1) * GROUP]) for g in range(groups)]
 
         pooled = []
+        inverse = []
         for i in range(images):
             at = slice(i * patches, (i + 1) * patches)
             found = []
+            inverse.append([])
             for g in range(groups):
                 cols = slice(g * GROUP, (g + 1) * GROUP)
                 to = slice(g * stacked, (g + 1) * stacked)
                 scores = dot_t(keys[at, cols], queries[g])
                 scores = jnp.exp(scores - jnp.max(scores, axis=0, keepdims=True))
-                scores = scores * (1.0 / jnp.sum(scores, axis=0, keepdims=True))
-                prob[at, to] = scores
+                inverse[i].append(1.0 / jnp.sum(scores, axis=0, keepdims=True))
                 weights = scores.astype(BF16)
-                prob_b[at, to] = weights
-                found.append(head_blocks(dot(values_t[cols, at], weights), block))
+                weights_ref[at, to] = weights
+                found.append(
+                    head_blocks(dot(values_t[cols, at], weights) * inverse[i][g], block)
+                )
             pooled.append(jnp.concatenate(found, axis=0).T.astype(BF16))
         mixed = dot(jnp.concatenate(pooled, axis=0), wo[...])
         caption_2 = jnp.concatenate([caption] * images, axis=0)
@@ -232,7 +301,8 @@
         slope = -LOGIT_SCALE * label / (1.0 + jnp.exp(label * logit))
         across = slope * mixed_inv * caption_inv
         grad_mixed = across * caption_2 - (slope * cosine * mixed_inv * mixed_inv) * mixed
-        grad_pooled = dot_t(grad_mixed.astype(BF16), wo[...]).astype(BF16)
+        by_caption = jnp.concatenate([head_columns(rows_, block) for rows_ in inverse], axis=0)
+        grad_pooled = (dot_t(grad_mixed.astype(BF16), wo[...]) * by_caption).astype(BF16)
         if own:
             direct = across * mixed - (slope * cosine * caption_inv * caption_inv) * caption_2
             direct = sum(direct[i * block : (i + 1) * block] for i in range(images))
@@ -246,11 +316,10 @@
                 at = slice(i * patches, (i + 1) * patches)
                 grads = head_stack(grad_pooled[i * block : (i + 1) * block, cols])
                 grad_weights = dot_t(values[at, cols], grads)
-                gv[at, cols] += dot(prob_b[at, to], grads)
-                weights = prob[at, to]
-                grad_scores = weights * (
-                    grad_weights - jnp.sum(weights * grad_weights, axis=0, keepdims=True)
-                )
+                gv[at, cols] += dot(weights_ref[at, to], grads)
+                weights = weights_ref[at, to].astype(F32)
+                mean = jnp.sum(weights * grad_weights, axis=0, keepdims=True) * inverse[i][g]
+                grad_scores = weights * (grad_weights - mean)
                 grad_scores = grad_scores.astype(BF16)
                 gk[at, cols] += dot(grad_scores, queries[g])
                 if own:
@@ -282,6 +351,7 @@
 
     for step in range(1, ns):
         span_copy(step, step).wait_recv()
+        span_owner_copy(step, step).wait_recv()
         run_all(step, False)
 
     gk_out[...] = gk[...].astype(BF16)
@@ -297,17 +367,32 @@
     @pl.loop(1, nb)
     def _(step):
         cap_copy(step, me).wait_send()
+        owner_copy(step, me).wait_send()
         part_copy(step, me).wait_send()
 
     for step in range(1, ns):
         span_copy(step, ns - step).wait_send()
-
-
-def token_kernel(patches, sum_ref, gk, gv, wk, wv, caption_out, token_out):
+        span_owner_copy(step, ns - step).wait_send()
+
+
+def token_kernel(patches, sum_ref, gk, gv, wk, wv, caption_out, token_out, made, sems):
     rows, d = caption_out.shape
+    total = gk.shape[0]
+    chunk = math.gcd(total, LANES)
+    copies = []
+    for n in range(total // chunk):
+        at = pl.ds(n * chunk, chunk)
+        made[at, :] = patches * (dot_t(gk[at, :], wk[...]) + dot_t(gv[at, :], wv[...]))
+        copies.append(pltpu.make_async_copy(made.at[at], token_out.at[at], sems.at[n]))
+        copies[-1].start()
     summed = sum_ref[...] * CAPTION_SCALE
     caption_out[...] = jnp.concatenate([summed[:rows], summed[rows:]], axis=1)
-    token_out[...] = patches * (dot_t(gk[...], wk[...]) + dot_t(gv[...], wv[...]))
+    for copy in copies:
+        copy.wait()
+
+
+def hold(x):
+    return pltpu.with_memory_space_constraint(x, pltpu.HBM)
 
 
 def on_device(nb, ns, image_tokens, captions, owner, w_query, w_key, w_value, w_out):
@@ -316,38 +401,44 @@
     total = images * patches
     block = math.gcd(nb * rows, LANES)
     vmem = pl.BlockSpec(memory_space=pltpu.VMEM)
-    anywhere = pl.BlockSpec(memory_space=pl.ANY)
+    hbm = pl.BlockSpec(memory_space=pltpu.HBM)
     heads = d // HEAD_DIM
     dma = pltpu.SemaphoreType.DMA
-    gk, gv, summed = pl.pallas_call(
+    gk, gv, summed, wk, wv = pl.pallas_call(
         functools.partial(pair_kernel, nb, ns, images),
         out_shape=(
             jax.ShapeDtypeStruct((total, d), BF16),
             jax.ShapeDtypeStruct((total, d), BF16),
             jax.ShapeDtypeStruct((2 * rows, d // 2), F32),
+            jax.ShapeDtypeStruct((d, d), BF16),
+            jax.ShapeDtypeStruct((d, d), BF16),
         ),
-        in_specs=[vmem, vmem] + [anywhere] * 5,
-        out_specs=(vmem, vmem, vmem),
+        in_specs=[hbm] * 7,
+        out_specs=(vmem,) * 5,
         scratch_shapes=[
+            pltpu.VMEM((rows, d), BF16),
+            pltpu.VMEM((1, rows), jnp.int32),
             pltpu.VMEM((total, d), BF16),
-            pltpu.VMEM((d, d), BF16),
-            pltpu.VMEM((d, d), BF16),
             pltpu.VMEM((d, d), BF16),
             pltpu.VMEM((d, d), BF16),
             pltpu.VMEM((total, d), BF16),
             pltpu.VMEM((total, d), BF16),
             pltpu.VMEM((d, total), BF16),
             pltpu.VMEM((d, total), BF16),
-            pltpu.VMEM((total, heads * block), F32),
             pltpu.VMEM((total, heads * block), BF16),
             pltpu.VMEM((total, d), F32),
             pltpu.VMEM((total, d), F32),
-            pltpu.VMEM((ns, nb, 2 * rows, d // 2 + LANES), BF16),
+            pltpu.VMEM((ns, nb, 2 * rows, d // 2), BF16),
+            pltpu.VMEM((ns, nb, 1, LANES), jnp.int32),
             pltpu.VMEM((nb, 2 * rows, d // 2), BF16),
             pltpu.VMEM((nb, 2 * rows, d // 2), BF16),
-            dma((5,)),
-            dma((nb,)),
-            dma((nb,)),
+            dma((7,)),
+            dma((nb,)),
+            dma((nb,)),
+            dma((nb,)),
+            dma((nb,)),
+            dma((ns,)),
+            dma((ns,)),
             dma((ns,)),
             dma((ns,)),
             dma((nb,)),
@@ -358,13 +449,13 @@
         ),
         name="pairs",
     )(
-        captions,
-        owner.reshape(rows, 1),
-        image_tokens.reshape(total, d),
-        w_query,
-        w_key,
-        w_value,
-        w_out,
+        hold(captions),
+        hold(owner.reshape(1, rows)),
+        hold(image_tokens.reshape(total, d)),
+        hold(w_query),
+        hold(w_key),
+        hold(w_value),
+        hold(w_out),
     )
     caption_grad, token_grad = pl.pallas_call(
         functools.partial(token_kernel, patches),
@@ -373,10 +464,14 @@
             jax.ShapeDtypeStruct((total, d), F32),
         ),
         in_specs=[vmem] * 5,
-        out_specs=(vmem, vmem),
+        out_specs=(vmem, hbm),
+        scratch_shapes=[
+            pltpu.VMEM((total, d), F32),
+            dma((total // math.gcd(total, LANES),)),
+        ],
         compiler_params=pltpu.CompilerParams(vmem_limit_bytes=16 * 2**20),
         name="token_grad",
-    )(summed, gk, gv, w_key, w_value)
+    )(summed, gk, gv, wk, wv)
     return (caption_grad, token_grad.reshape(images, patches, d))
 
 

time: 30.9 us -> 25.2 us (0.82)
  local copies, waits for them, and re-layouts: 5.95 us -> 0 us
  Pallas kernels: 23.9 us -> 24.4 us
    unnamed x12 -> x0, local copies, waits for them, and re-layouts: 5.21 us -> none
    pallas_call x1, Pallas kernels: 1.72 us -> 2.81 us  [on_device(): pl.pallas_call(functools.partial(token_kernel, patches), out_shape=(jax.S...]
    reshape x1 -> x0, local copies, waits for them, and re-layouts: 0.74 us -> none  [on_device(): owner.reshape(rows, 1)]
    pallas_call x1, Pallas kernels: 22.1 us -> 21.6 us  [on_device(): pl.pallas_call(functools.partial(pair_kernel, nb, ns, images), out_shape=...]
where the time goes in v2:
time: 25.2 us; the launch traced here: 25 us
  Pallas kernels  24.4 us (97%)
  between operations  0.64 us (3%)
    pallas_call x1, Pallas kernels, on_device(): pl.pallas_call(functools.partial(pair_kernel, nb, ns, images), out_shape=...  21.6 us
    pallas_call x1, Pallas kernels, on_device(): pl.pallas_call(functools.partial(token_kernel, patches), out_shape=(jax.S...  2.81 us

profile of v2, /device:TPU:0, one launch (start us, length us, event | category | flops | bytes accessed | tf_op | source)
XLA Modules:
  0.0 25.0 jit_solution(5059469155749649396)
XLA Ops:
  0.6 21.6 %pairs.1 = (bf16[512,512]{1,0:T(8,128)(2,1)S(1)}, bf16[512,512]{1,0:T(8,128)(2,1)S(1)}, f32[16,256]{1,0:T(8,128)S(1)}, bf16[512,512]{1,0:T(8,128)(2,1)S(1)}, bf16[512,512]{1,0:T(8,128)(2,1)S(1)}) custom-call(bf16[8,512]{1,0:T(8,128)(2,1)} %captions_hbm.1, s32[1,8]{1,0:T(1,128)} %bitcast.4, bf16[512,512]{1,0:T(8,128)(2,1)} %bitcast.3, ...), custom_call_target="tpu_custom_call" | custom-call | tf_op jit(solution)/shard_map/pairs/pallas_call | solution.py:407
  22.2 2.8 %token_grad.1 = (f32[8,512]{1,0:T(8,128)}, f32[512,512]{1,0:T(8,128)}) custom-call(f32[16,256]{1,0:T(8,128)S(1)} %get-tuple-element.9.sum_ref, bf16[512,512]{1,0:T(8,128)(2,1)S(1)} %get-tuple-element.10.gk, bf16[512,512]{1,0:T(8,128)(2,1)S(1)} %get-tuple-element.11.gv, bf16[512,512]{1,0:T(8,128)(2,1)S(1)} %get-tuple-element.12.wk, ...), custom_call_target="tpu_custom_call" | custom-call | tf_op jit(solution)/shard_map/token_grad/pallas_call | solution.py:460

commit v3 on v2

--- a/solution.py
+++ b/solution.py
@@ -110,6 +110,7 @@
     slots = block // rows
     blocks = nb * rows // block
     stacked = HEADS_IN_GROUP * block
+    unroll = nb <= 16
 
     def peer_of(step):
         return lax.rem(me + step, nb)
@@ -136,7 +137,7 @@
 
     barrier = pltpu.get_barrier_semaphore()
 
-    @pl.loop(1, nb)
+    @pl.loop(1, nb, unroll=unroll)
     def _(step):
         pl.semaphore_signal(
             barrier, inc=1, device_id={"batch": peer_of(step)}, device_id_type=MESH
@@ -159,32 +160,32 @@
 
     pl.semaphore_wait(barrier, nb + ns - 2)
 
-    def cap_copy(step, slot):
+    def cap_copy(step):
         return pltpu.make_async_remote_copy(
             src_ref=caps.at[0, me],
             dst_ref=caps.at[0, me],
-            send_sem=cap_send.at[step],
-            recv_sem=cap_recv.at[slot],
+            send_sem=cap_send,
+            recv_sem=cap_recv,
             device_id={"batch": peer_of(step)},
             device_id_type=MESH,
         )
 
-    def owner_copy(step, slot):
+    def owner_copy(step):
         return pltpu.make_async_remote_copy(
             src_ref=owners.at[0, me],
             dst_ref=owners.at[0, me],
-            send_sem=owner_send.at[step],
-            recv_sem=owner_recv.at[slot],
+            send_sem=owner_send,
+            recv_sem=owner_recv,
             device_id={"batch": peer_of(step)},
             device_id_type=MESH,
         )
 
-    def part_copy(step, slot):
+    def part_copy(step):
         return pltpu.make_async_remote_copy(
             src_ref=part.at[peer_of(step)],
             dst_ref=parts_in.at[me],
-            send_sem=part_send.at[step],
-            recv_sem=part_recv.at[slot],
+            send_sem=part_send,
+            recv_sem=part_recv,
             device_id={"batch": peer_of(step)},
             device_id_type=MESH,
         )
@@ -199,6 +200,20 @@
             device_id_type=MESH,
         )
 
+    def whole(ref, send_sem, recv_sem):
+        return pltpu.make_async_remote_copy(
+            src_ref=ref.at[pl.ds(0, nb - 1)],
+            dst_ref=ref.at[pl.ds(0, nb - 1)],
+            send_sem=send_sem,
+            recv_sem=recv_sem,
+            device_id={"batch": peer_of(1)},
+            device_id_type=MESH,
+        )
+
+    all_caps = whole(caps.at[0], cap_send, cap_recv)
+    all_owners = whole(owners.at[0], owner_send, owner_recv)
+    all_parts = whole(parts_in, part_send, part_recv)
+
     def span_owner_copy(step, slot):
         return pltpu.make_async_remote_copy(
             src_ref=owners.at[0],
@@ -209,13 +224,13 @@
             device_id_type=MESH,
         )
 
-    @pl.loop(1, nb)
+    @pl.loop(1, nb, unroll=unroll)
     def _(step):
-        cap_copy(step, me).start()
-
-    @pl.loop(1, nb)
+        cap_copy(step).start()
+
+    @pl.loop(1, nb, unroll=unroll)
     def _(step):
-        owner_copy(step, me).start()
+        owner_copy(step).start()
 
     for load in loads[2:5]:
         load.wait()
@@ -227,26 +242,32 @@
         found = dot(tokens[at, :], wv[...])
         values[at, :] = found.astype(BF16)
         values_t[:, at] = found.T.astype(BF16)
-    gk[...] = jnp.zeros_like(gk)
-    gv[...] = jnp.zeros_like(gv)
+    if blocks > 1:
+        gk[...] = jnp.zeros_like(gk)
+        gv[...] = jnp.zeros_like(gv)
     for load in loads[5:]:
         load.wait()
 
-    @pl.loop(1, nb)
-    def _(step):
-        cap_copy(step, peer_of(step)).wait_recv()
+    all_caps.wait_recv()
 
     for step in range(1, ns):
         span_copy(step, ns - step).start()
 
-    @pl.loop(1, nb)
-    def _(step):
-        owner_copy(step, peer_of(step)).wait_recv()
+    all_owners.wait_recv()
 
     for step in range(1, ns):
         span_owner_copy(step, ns - step).start()
 
+    def add(total, out, at, cols, found, which):
+        if blocks > 1 or which > 0:
+            found = total[at, cols] + found
+        if blocks == 1 and which == ns - 1:
+            out[at, cols] = found.astype(BF16)
+        else:
+            total[at, cols] = found
+
     def run_block(slot, which, own):
+        later = []
         held = caps[which, pl.ds(slot, slots)].astype(F32)
         caption = jnp.concatenate(
             [
@@ -280,7 +301,7 @@
                 scores = jnp.exp(scores - jnp.max(scores, axis=0, keepdims=True))
                 inverse[i].append(1.0 / jnp.sum(scores, axis=0, keepdims=True))
                 weights = scores.astype(BF16)
-                weights_ref[at, to] = weights
+                weights_ref[which, at, to] = weights
                 found.append(
                     head_blocks(dot(values_t[cols, at], weights) * inverse[i][g], block)
                 )
@@ -316,12 +337,15 @@
                 at = slice(i * patches, (i + 1) * patches)
                 grads = head_stack(grad_pooled[i * block : (i + 1) * block, cols])
                 grad_weights = dot_t(values[at, cols], grads)
-                gv[at, cols] += dot(weights_ref[at, to], grads)
-                weights = weights_ref[at, to].astype(F32)
+                weights = weights_ref[which, at, to].astype(F32)
                 mean = jnp.sum(weights * grad_weights, axis=0, keepdims=True) * inverse[i][g]
                 grad_scores = weights * (grad_weights - mean)
                 grad_scores = grad_scores.astype(BF16)
-                gk[at, cols] += dot(grad_scores, queries[g])
+                later.append(
+                    functools.partial(
+                        finish, at, cols, to, grads, grad_scores, queries[g], which
+                    )
+                )
                 if own:
                     found = head_blocks(dot(keys_t[cols, at], grad_scores), block)
                     total = found if total is None else total + found
@@ -333,42 +357,49 @@
             part[pl.ds(slot, slots)] = jnp.concatenate(
                 [grad[:, :, :half], grad[:, :, half:]], axis=1
             ).astype(BF16)
+        return later
+
+    def finish(at, cols, to, grads, grad_scores, queries, which):
+        add(gv, gv_out, at, cols, dot(weights_ref[which, at, to], grads), which)
+        add(gk, gk_out, at, cols, dot(grad_scores, queries), which)
 
     def run_all(which, own):
         if blocks == 1:
-            run_block(0, which, own)
-        else:
-
-            @pl.loop(0, blocks)
-            def _(n):
-                run_block(n * slots, which, own)
-
-    run_all(0, True)
-
-    @pl.loop(1, nb)
+            return run_block(0, which, own)
+
+        @pl.loop(0, blocks)
+        def _(n):
+            for work in run_block(n * slots, which, own):
+                work()
+
+        return []
+
+    later = run_all(0, True)
+
+    @pl.loop(1, nb, unroll=unroll)
     def _(step):
-        part_copy(step, me).start()
+        part_copy(step).start()
 
     for step in range(1, ns):
         span_copy(step, step).wait_recv()
         span_owner_copy(step, step).wait_recv()
-        run_all(step, False)
-
-    gk_out[...] = gk[...].astype(BF16)
-    gv_out[...] = gv[...].astype(BF16)
-
-    @pl.loop(1, nb)
-    def _(step):
-        part_copy(step, peer_of(step)).wait_recv()
+        for work in later:
+            work()
+        later = run_all(step, False)
+    for work in later:
+        work()
+    if blocks > 1:
+        gk_out[...] = gk[...].astype(BF16)
+        gv_out[...] = gv[...].astype(BF16)
+
+    all_parts.wait_recv()
 
     parts_in[me] = part[me]
     sum_out[...] = jnp.sum(parts_in[...].astype(F32), axis=0)
 
-    @pl.loop(1, nb)
-    def _(step):
-        cap_copy(step, me).wait_send()
-        owner_copy(step, me).wait_send()
-        part_copy(step, me).wait_send()
+    all_caps.wait_send()
+    all_owners.wait_send()
+    all_parts.wait_send()
 
     for step in range(1, ns):
         span_copy(step, ns - step).wait_send()
@@ -377,13 +408,11 @@
 
 def token_kernel(patches, sum_ref, gk, gv, wk, wv, caption_out, token_out, made, sems):
     rows, d = caption_out.shape
-    total = gk.shape[0]
-    chunk = math.gcd(total, LANES)
     copies = []
-    for n in range(total // chunk):
-        at = pl.ds(n * chunk, chunk)
-        made[at, :] = patches * (dot_t(gk[at, :], wk[...]) + dot_t(gv[at, :], wv[...]))
-        copies.append(pltpu.make_async_copy(made.at[at], token_out.at[at], sems.at[n]))
+    for n in range(d // GROUP):
+        at = pl.ds(n * GROUP, GROUP)
+        made[:, at] = patches * (dot_t(gk[...], wk[at, :]) + dot_t(gv[...], wv[at, :]))
+        copies.append(pltpu.make_async_copy(made.at[:, at], token_out.at[:, at], sems.at[n]))
         copies[-1].start()
     summed = sum_ref[...] * CAPTION_SCALE
     caption_out[...] = jnp.concatenate([summed[:rows], summed[rows:]], axis=1)
@@ -425,7 +454,7 @@
             pltpu.VMEM((total, d), BF16),
             pltpu.VMEM((d, total), BF16),
             pltpu.VMEM((d, total), BF16),
-            pltpu.VMEM((total, heads * block), BF16),
+            pltpu.VMEM((ns, total, heads * block), BF16),
             pltpu.VMEM((total, d), F32),
             pltpu.VMEM((total, d), F32),
             pltpu.VMEM((ns, nb, 2 * rows, d // 2), BF16),
@@ -433,16 +462,16 @@
             pltpu.VMEM((nb, 2 * rows, d // 2), BF16),
             pltpu.VMEM((nb, 2 * rows, d // 2), BF16),
             dma((7,)),
-            dma((nb,)),
-            dma((nb,)),
-            dma((nb,)),
-            dma((nb,)),
+            dma,
+            dma,
+            dma,
+            dma,
             dma((ns,)),
             dma((ns,)),
             dma((ns,)),
             dma((ns,)),
-            dma((nb,)),
-            dma((nb,)),
+            dma,
+            dma,
         ],
         compiler_params=pltpu.CompilerParams(
             collective_id=0, has_side_effects=True, vmem_limit_bytes=36 * 2**20
@@ -467,7 +496,7 @@
         out_specs=(vmem, hbm),
         scratch_shapes=[
             pltpu.VMEM((total, d), F32),
-            dma((total // math.gcd(total, LANES),)),
+            dma((d // GROUP,)),
         ],
         compiler_params=pltpu.CompilerParams(vmem_limit_bytes=16 * 2**20),
         name="token_grad",

time: 25.2 us -> 23.5 us (0.933)
  Pallas kernels: 24.4 us -> 22.7 us
    pallas_call x1, Pallas kernels: 21.6 us -> 20.4 us  [on_device(): pl.pallas_call(functools.partial(pair_kernel, nb, ns, images), out_shape=...]
    pallas_call x1, Pallas kernels: 2.81 us -> 2.32 us  [on_device(): pl.pallas_call(functools.partial(token_kernel, patches), out_shape=(jax.S...]
where the time goes in v3:
time: 23.5 us; the launch traced here: 23.3 us
  Pallas kernels  22.7 us (97%)
  between operations  0.64 us (3%)
    pallas_call x1, Pallas kernels, on_device(): pl.pallas_call(functools.partial(pair_kernel, nb, ns, images), out_shape=...  20.4 us
    pallas_call x1, Pallas kernels, on_device(): pl.pallas_call(functools.partial(token_kernel, patches), out_shape=(jax.S...  2.32 us

profile of v3, /device:TPU:0, one launch (start us, length us, event | category | flops | bytes accessed | tf_op | source)
XLA Modules:
  0.0 23.3 jit_solution(15268294748152783950)
XLA Ops:
  0.6 20.4 %pairs.1 = (bf16[512,512]{1,0:T(8,128)(2,1)S(1)}, bf16[512,512]{1,0:T(8,128)(2,1)S(1)}, f32[16,256]{1,0:T(8,128)S(1)}, bf16[512,512]{1,0:T(8,128)(2,1)S(1)}, bf16[512,512]{1,0:T(8,128)(2,1)S(1)}) custom-call(bf16[8,512]{1,0:T(8,128)(2,1)} %captions_hbm.1, s32[1,8]{1,0:T(1,128)} %bitcast.4, bf16[512,512]{1,0:T(8,128)(2,1)} %bitcast.3, ...), custom_call_target="tpu_custom_call" | custom-call | tf_op jit(solution)/shard_map/pairs/pallas_call | solution.py:436
  21.0 2.3 %token_grad.1 = (f32[8,512]{1,0:T(8,128)}, f32[512,512]{1,0:T(8,128)}) custom-call(f32[16,256]{1,0:T(8,128)S(1)} %get-tuple-element.9.sum_ref, bf16[512,512]{1,0:T(8,128)(2,1)S(1)} %get-tuple-element.10.gk, bf16[512,512]{1,0:T(8,128)(2,1)S(1)} %get-tuple-element.11.gv, bf16[512,512]{1,0:T(8,128)(2,1)S(1)} %get-tuple-element.12.wk, ...), custom_call_target="tpu_custom_call" | custom-call | tf_op jit(solution)/shard_map/token_grad/pallas_call | solution.py:489

commit v4 on v3

--- a/solution.py
+++ b/solution.py
@@ -29,11 +29,15 @@
     return lax.dot_general(a, b, (((1,), (1,)), ((), ())), preferred_element_type=F32)
 
 
+def head_masks(tile):
+    head = lax.broadcasted_iota(jnp.int32, (tile, GROUP), 1) // HEAD_DIM
+    return [(head == h).astype(F32).astype(BF16) for h in range(HEADS_IN_GROUP)]
+
+
 def head_stack(x):
-    head = lax.broadcasted_iota(jnp.int32, x.shape, 1) // HEAD_DIM
-    return jnp.concatenate(
-        [jnp.where(head == h, x, jnp.zeros_like(x)) for h in range(HEADS_IN_GROUP)], axis=0
-    )
+    tile = math.gcd(x.shape[0], 16)
+    tiles = x.reshape(x.shape[0] // tile, tile, GROUP)
+    return jnp.concatenate([(tiles * m).reshape(x.shape) for m in head_masks(tile)], axis=0)
 
 
 def head_blocks(x, width):
@@ -238,10 +242,10 @@
         at = pl.ds(i * patches, patches)
         found = dot(tokens[at, :], wk[...])
         keys[at, :] = found.astype(BF16)
-        keys_t[:, at] = found.T.astype(BF16)
+        keys_t[:, at] = found.astype(BF16).T
         found = dot(tokens[at, :], wv[...])
         values[at, :] = found.astype(BF16)
-        values_t[:, at] = found.T.astype(BF16)
+        values_t[:, at] = found.astype(BF16).T
     if blocks > 1:
         gk[...] = jnp.zeros_like(gk)
         gv[...] = jnp.zeros_like(gv)
@@ -266,7 +270,7 @@
         else:
             total[at, cols] = found
 
-    def run_block(slot, which, own):
+    def run_block(slot, which, own, before=()):
         later = []
         held = caps[which, pl.ds(slot, slots)].astype(F32)
         caption = jnp.concatenate(
@@ -288,24 +292,35 @@
         query = (dot(caption.astype(BF16), wq[...]) * HEAD_DIM**-0.5).astype(BF16)
         queries = [head_stack(query[:, g * GROUP : (g + 1) * GROUP]) for g in range(groups)]
 
-        pooled = []
-        inverse = []
-        for i in range(images):
-            at = slice(i * patches, (i + 1) * patches)
-            found = []
-            inverse.append([])
-            for g in range(groups):
-                cols = slice(g * GROUP, (g + 1) * GROUP)
-                to = slice(g * stacked, (g + 1) * stacked)
-                scores = dot_t(keys[at, cols], queries[g])
-                scores = jnp.exp(scores - jnp.max(scores, axis=0, keepdims=True))
-                inverse[i].append(1.0 / jnp.sum(scores, axis=0, keepdims=True))
-                weights = scores.astype(BF16)
-                weights_ref[which, at, to] = weights
-                found.append(
-                    head_blocks(dot(values_t[cols, at], weights) * inverse[i][g], block)
-                )
-            pooled.append(jnp.concatenate(found, axis=0).T.astype(BF16))
+        units = [(i, g) for i in range(images) for g in range(groups)]
+
+        def places(i, g):
+            return (
+                slice(i * patches, (i + 1) * patches),
+                slice(g * GROUP, (g + 1) * GROUP),
+                slice(g * stacked, (g + 1) * stacked),
+            )
+
+        def score(i, g):
+            at, cols, _ = places(i, g)
+            return dot_t(keys[at, cols], queries[g])
+
+        pooled = [[] for _ in range(images)]
+        inverse = [[] for _ in range(images)]
+        ahead = score(*units[0])
+        for n, (i, g) in enumerate(units):
+            at, cols, to = places(i, g)
+            scores = ahead
+            if n + 1 < len(units):
+                ahead = score(*units[n + 1])
+            if n < len(before):
+                before[n]()
+            scores = jnp.exp(scores - jnp.max(scores, axis=0, keepdims=True))
+            inverse[i].append(1.0 / jnp.sum(scores, axis=0, keepdims=True))
+            weights = scores.astype(BF16)
+            weights_ref[which, at, to] = weights
+            pooled[i].append(head_blocks(dot(values_t[cols, at], weights) * inverse[i][g], block))
+        pooled = [jnp.concatenate(found, axis=0).T.astype(BF16) for found in pooled]
         mixed = dot(jnp.concatenate(pooled, axis=0), wo[...])
         caption_2 = jnp.concatenate([caption] * images, axis=0)
         owner_2 = jnp.concatenate([owner] * images, axis=0)
@@ -328,28 +343,29 @@
             direct = across * mixed - (slope * cosine * caption_inv * caption_inv) * caption_2
             direct = sum(direct[i * block : (i + 1) * block] for i in range(images))
 
-        grad_query = []
-        for g in range(groups):
-            cols = slice(g * GROUP, (g + 1) * GROUP)
-            to = slice(g * stacked, (g + 1) * stacked)
-            total = None
-            for i in range(images):
-                at = slice(i * patches, (i + 1) * patches)
-                grads = head_stack(grad_pooled[i * block : (i + 1) * block, cols])
-                grad_weights = dot_t(values[at, cols], grads)
-                weights = weights_ref[which, at, to].astype(F32)
-                mean = jnp.sum(weights * grad_weights, axis=0, keepdims=True) * inverse[i][g]
-                grad_scores = weights * (grad_weights - mean)
-                grad_scores = grad_scores.astype(BF16)
-                later.append(
-                    functools.partial(
-                        finish, at, cols, to, grads, grad_scores, queries[g], which
-                    )
-                )
-                if own:
-                    found = head_blocks(dot(keys_t[cols, at], grad_scores), block)
-                    total = found if total is None else total + found
-            grad_query.append(total)
+        def grad_weight(i, g):
+            at, cols, _ = places(i, g)
+            grads = head_stack(grad_pooled[i * block : (i + 1) * block, cols])
+            return grads, dot_t(values[at, cols], grads)
+
+        grad_query = [None] * groups
+        ahead = grad_weight(*units[0])
+        for n, (i, g) in enumerate(units):
+            at, cols, to = places(i, g)
+            grads, grad_weights = ahead
+            if n + 1 < len(units):
+                ahead = grad_weight(*units[n + 1])
+            weights = weights_ref[which, at, to].astype(F32)
+            mean = jnp.sum(weights * grad_weights, axis=0, keepdims=True) * inverse[i][g]
+            grad_scores = (weights * (grad_weights - mean)).astype(BF16)
+            later.append(
+                functools.partial(finish, at, cols, to, grads, grad_scores, queries[g], which)
+            )
+            if own:
+                found = head_blocks(dot(keys_t[cols, at], grad_scores), block)
+                grad_query[g] = found if grad_query[g] is None else grad_query[g] + found
+            else:
+                later.pop()()
         if own:
             grad_query = jnp.concatenate(grad_query, axis=0).T * HEAD_DIM**-0.5
             grad = direct + dot_t(grad_query.astype(BF16), wq[...])
@@ -363,9 +379,9 @@
         add(gv, gv_out, at, cols, dot(weights_ref[which, at, to], grads), which)
         add(gk, gk_out, at, cols, dot(grad_scores, queries), which)
 
-    def run_all(which, own):
+    def run_all(which, own, before=()):
         if blocks == 1:
-            return run_block(0, which, own)
+            return run_block(0, which, own, before)
 
         @pl.loop(0, blocks)
         def _(n):
@@ -383,9 +399,7 @@
     for step in range(1, ns):
         span_copy(step, step).wait_recv()
         span_owner_copy(step, step).wait_recv()
-        for work in later:
-            work()
-        later = run_all(step, False)
+        later = run_all(step, False, later)
     for work in later:
         work()
     if blocks > 1:
@@ -406,16 +420,17 @@
         span_owner_copy(step, ns - step).wait_send()
 
 
-def token_kernel(patches, sum_ref, gk, gv, wk, wv, caption_out, token_out, made, sems):
+def token_kernel(patches, sum_ref, gk, gv, wk, wv, caption_out, token_out, unfolded, made, sems):
     rows, d = caption_out.shape
-    copies = []
+    summed = sum_ref[...] * CAPTION_SCALE
+    unfolded[...] = jnp.concatenate([summed[:rows], summed[rows:]], axis=1)
+    copies = [pltpu.make_async_copy(unfolded, caption_out, sems.at[0])]
+    copies[0].start()
     for n in range(d // GROUP):
         at = pl.ds(n * GROUP, GROUP)
         made[:, at] = patches * (dot_t(gk[...], wk[at, :]) + dot_t(gv[...], wv[at, :]))
-        copies.append(pltpu.make_async_copy(made.at[:, at], token_out.at[:, at], sems.at[n]))
+        copies.append(pltpu.make_async_copy(made.at[:, at], token_out.at[:, at], sems.at[n + 1]))
         copies[-1].start()
-    summed = sum_ref[...] * CAPTION_SCALE
-    caption_out[...] = jnp.concatenate([summed[:rows], summed[rows:]], axis=1)
     for copy in copies:
         copy.wait()
 
@@ -493,10 +508,11 @@
             jax.ShapeDtypeStruct((total, d), F32),
         ),
         in_specs=[vmem] * 5,
-        out_specs=(vmem, hbm),
+        out_specs=(hbm, hbm),
         scratch_shapes=[
+            pltpu.VMEM((rows, d), F32),
             pltpu.VMEM((total, d), F32),
-            dma((d // GROUP,)),
+            dma((d // GROUP + 1,)),
         ],
         compiler_params=pltpu.CompilerParams(vmem_limit_bytes=16 * 2**20),
         name="token_grad",

time: 23.5 us -> 22 us (0.936)
  Pallas kernels: 22.7 us -> 21.2 us
    pallas_call x1, Pallas kernels: 20.4 us -> 19.4 us  [on_device(): pl.pallas_call(functools.partial(pair_kernel, nb, ns, images), out_shape=...]
    pallas_call x1, Pallas kernels: 2.32 us -> 1.73 us  [on_device(): pl.pallas_call(functools.partial(token_kernel, patches), out_shape=(jax.S...]
where the time goes in v4:
time: 22 us; the launch traced here: 21.8 us
  Pallas kernels  21.2 us (96%)
  between operations  0.64 us (3%)
    pallas_call x1, Pallas kernels, on_device(): pl.pallas_call(functools.partial(pair_kernel, nb, ns, images), out_shape=...  19.4 us
    pallas_call x1, Pallas kernels, on_device(): pl.pallas_call(functools.partial(token_kernel, patches), out_shape=(jax.S...  1.73 us

profile of v4, /device:TPU:0, one launch (start us, length us, event | category | flops | bytes accessed | tf_op | source)
XLA Modules:
  0.0 21.8 jit_solution(5733054567445364094)
XLA Ops:
  0.6 19.4 %pairs.1 = (bf16[512,512]{1,0:T(8,128)(2,1)S(1)}, bf16[512,512]{1,0:T(8,128)(2,1)S(1)}, f32[16,256]{1,0:T(8,128)S(1)}, bf16[512,512]{1,0:T(8,128)(2,1)S(1)}, bf16[512,512]{1,0:T(8,128)(2,1)S(1)}) custom-call(bf16[8,512]{1,0:T(8,128)(2,1)} %captions_hbm.1, s32[1,8]{1,0:T(1,128)} %bitcast.4, bf16[512,512]{1,0:T(8,128)(2,1)} %bitcast.3, ...), custom_call_target="tpu_custom_call" | custom-call | tf_op jit(solution)/shard_map/pairs/pallas_call | solution.py:451
  20.1 1.7 %token_grad.1 = (f32[8,512]{1,0:T(8,128)}, f32[512,512]{1,0:T(8,128)}) custom-call(f32[16,256]{1,0:T(8,128)S(1)} %get-tuple-element.9.sum_ref, bf16[512,512]{1,0:T(8,128)(2,1)S(1)} %get-tuple-element.10.gk, bf16[512,512]{1,0:T(8,128)(2,1)S(1)} %get-tuple-element.11.gv, bf16[512,512]{1,0:T(8,128)(2,1)S(1)} %get-tuple-element.12.wk, ...), custom_call_target="tpu_custom_call" | custom-call | tf_op jit(solution)/shard_map/token_grad/pallas_call | solution.py:504

commit v5 on v4

--- a/solution.py
+++ b/solution.py
@@ -50,13 +50,8 @@
     )
 
 
-def head_columns(parts, width):
-    parts = [
-        part[:, h * width : (h + 1) * width] for part in parts for h in range(HEADS_IN_GROUP)
-    ]
-    return jnp.concatenate(
-        [jnp.broadcast_to(part, (HEAD_DIM, width)) for part in parts], axis=0
-    ).T
+def by_head(rows, width):
+    return [rows[:, h * width : (h + 1) * width] for h in range(HEADS_IN_GROUP)]
 
 
 def pair_kernel(
@@ -70,15 +65,14 @@
     wk_hbm,
     wv_hbm,
     wo_hbm,
-    gk_out,
-    gv_out,
+    token_out,
     sum_out,
-    wk,
-    wv,
     captions_ref,
     owner_ref,
     tokens,
     wq,
+    wk,
+    wv,
     wo,
     keys,
     values,
@@ -87,6 +81,8 @@
     weights_ref,
     gk,
     gv,
+    gk_b,
+    gv_b,
     caps,
     owners,
     part,
@@ -320,6 +316,7 @@
             weights = scores.astype(BF16)
             weights_ref[which, at, to] = weights
             pooled[i].append(head_blocks(dot(values_t[cols, at], weights) * inverse[i][g], block))
+        pooled_t = pooled
         pooled = [jnp.concatenate(found, axis=0).T.astype(BF16) for found in pooled]
         mixed = dot(jnp.concatenate(pooled, axis=0), wo[...])
         caption_2 = jnp.concatenate([caption] * images, axis=0)
@@ -337,15 +334,41 @@
         slope = -LOGIT_SCALE * label / (1.0 + jnp.exp(label * logit))
         across = slope * mixed_inv * caption_inv
         grad_mixed = across * caption_2 - (slope * cosine * mixed_inv * mixed_inv) * mixed
-        by_caption = jnp.concatenate([head_columns(rows_, block) for rows_ in inverse], axis=0)
-        grad_pooled = (dot_t(grad_mixed.astype(BF16), wo[...]) * by_caption).astype(BF16)
+        grad_pooled_t = dot_t(wo[...], grad_mixed.astype(BF16))
         if own:
             direct = across * mixed - (slope * cosine * caption_inv * caption_inv) * caption_2
             direct = sum(direct[i * block : (i + 1) * block] for i in range(images))
 
+        grad_pooled = []
+        means = []
+        for i in range(images):
+            scale = jnp.concatenate(
+                [
+                    jnp.broadcast_to(row, (HEAD_DIM, block))
+                    for rows_ in inverse[i]
+                    for row in by_head(rows_, block)
+                ],
+                axis=0,
+            )
+            found = (grad_pooled_t[:, i * block : (i + 1) * block] * scale).astype(BF16)
+            grad_pooled.append(found.T)
+            products = found.astype(F32) * jnp.concatenate(pooled_t[i], axis=0)
+            products = [
+                jnp.sum(products[h * HEAD_DIM : (h + 1) * HEAD_DIM], axis=0, keepdims=True)
+                for h in range(d // HEAD_DIM)
+            ]
+            means.append(
+                [
+                    jnp.concatenate(
+                        products[g * HEADS_IN_GROUP : (g + 1) * HEADS_IN_GROUP], axis=1
+                    )
+                    for g in range(groups)
+                ]
+            )
+
         def grad_weight(i, g):
             at, cols, _ = places(i, g)
-            grads = head_stack(grad_pooled[i * block : (i + 1) * block, cols])
+            grads = head_stack(grad_pooled[i][:, cols])
             return grads, dot_t(values[at, cols], grads)
 
         grad_query = [None] * groups
@@ -356,8 +379,7 @@
             if n + 1 < len(units):
                 ahead = grad_weight(*units[n + 1])
             weights = weights_ref[which, at, to].astype(F32)
-            mean = jnp.sum(weights * grad_weights, axis=0, keepdims=True) * inverse[i][g]
-            grad_scores = (weights * (grad_weights - mean)).astype(BF16)
+            grad_scores = (weights * (grad_weights - means[i][g])).astype(BF16)
             later.append(
                 functools.partial(finish, at, cols, to, grads, grad_scores, queries[g], which)
             )
@@ -366,6 +388,8 @@
                 grad_query[g] = found if grad_query[g] is None else grad_query[g] + found
             else:
                 later.pop()()
+                if blocks == 1 and which == ns - 1 and g == groups - 1:
+                    token_product(at)
         if own:
             grad_query = jnp.concatenate(grad_query, axis=0).T * HEAD_DIM**-0.5
             grad = direct + dot_t(grad_query.astype(BF16), wq[...])
@@ -375,9 +399,12 @@
             ).astype(BF16)
         return later
 
+    def token_product(at):
+        token_out[at, :] = patches * (dot_t(gk_b[at, :], wk[...]) + dot_t(gv_b[at, :], wv[...]))
+
     def finish(at, cols, to, grads, grad_scores, queries, which):
-        add(gv, gv_out, at, cols, dot(weights_ref[which, at, to], grads), which)
-        add(gk, gk_out, at, cols, dot(grad_scores, queries), which)
+        add(gv, gv_b, at, cols, dot(weights_ref[which, at, to], grads), which)
+        add(gk, gk_b, at, cols, dot(grad_scores, queries), which)
 
     def run_all(which, own, before=()):
         if blocks == 1:
@@ -403,8 +430,11 @@
     for work in later:
         work()
     if blocks > 1:
-        gk_out[...] = gk[...].astype(BF16)
-        gv_out[...] = gv[...].astype(BF16)
+        gk_b[...] = gk[...].astype(BF16)
+        gv_b[...] = gv[...].astype(BF16)
+    if blocks > 1 or ns == 1:
+        for i in range(images):
+            token_product(slice(i * patches, (i + 1) * patches))
 
     all_parts.wait_recv()
 
@@ -420,17 +450,24 @@
         span_owner_copy(step, ns - step).wait_send()
 
 
-def token_kernel(patches, sum_ref, gk, gv, wk, wv, caption_out, token_out, unfolded, made, sems):
+def write_kernel(sum_ref, token_ref, caption_out, token_out, unfolded, sems):
     rows, d = caption_out.shape
+    count = sems.shape[0] - 1
+    chunk = token_ref.shape[0] // count
+    copies = [
+        pltpu.make_async_copy(
+            token_ref.at[pl.ds(n * chunk, chunk)],
+            token_out.at[pl.ds(n * chunk, chunk)],
+            sems.at[n],
+        )
+        for n in range(count)
+    ]
+    for copy in copies:
+        copy.start()
     summed = sum_ref[...] * CAPTION_SCALE
     unfolded[...] = jnp.concatenate([summed[:rows], summed[rows:]], axis=1)
-    copies = [pltpu.make_async_copy(unfolded, caption_out, sems.at[0])]
-    copies[0].start()
-    for n in range(d // GROUP):
-        at = pl.ds(n * GROUP, GROUP)
-        made[:, at] = patches * (dot_t(gk[...], wk[at, :]) + dot_t(gv[...], wv[at, :]))
-        copies.append(pltpu.make_async_copy(made.at[:, at], token_out.at[:, at], sems.at[n + 1]))
-        copies[-1].start()
+    copies.append(pltpu.make_async_copy(unfolded, caption_out, sems.at[count]))
+    copies[-1].start()
     for copy in copies:
         copy.wait()
 
@@ -448,21 +485,20 @@
     hbm = pl.BlockSpec(memory_space=pltpu.HBM)
     heads = d // HEAD_DIM
     dma = pltpu.SemaphoreType.DMA
-    gk, gv, summed, wk, wv = pl.pallas_call(
+    token_terms, summed = pl.pallas_call(
         functools.partial(pair_kernel, nb, ns, images),
         out_shape=(
-            jax.ShapeDtypeStruct((total, d), BF16),
-            jax.ShapeDtypeStruct((total, d), BF16),
+            jax.ShapeDtypeStruct((total, d), F32),
             jax.ShapeDtypeStruct((2 * rows, d // 2), F32),
-            jax.ShapeDtypeStruct((d, d), BF16),
-            jax.ShapeDtypeStruct((d, d), BF16),
         ),
         in_specs=[hbm] * 7,
-        out_specs=(vmem,) * 5,
+        out_specs=(vmem, vmem),
         scratch_shapes=[
             pltpu.VMEM((rows, d), BF16),
             pltpu.VMEM((1, rows), jnp.int32),
             pltpu.VMEM((total, d), BF16),
+            pltpu.VMEM((d, d), BF16),
+            pltpu.VMEM((d, d), BF16),
             pltpu.VMEM((d, d), BF16),
             pltpu.VMEM((d, d), BF16),
             pltpu.VMEM((total, d), BF16),
@@ -472,6 +508,8 @@
             pltpu.VMEM((ns, total, heads * block), BF16),
             pltpu.VMEM((total, d), F32),
             pltpu.VMEM((total, d), F32),
+            pltpu.VMEM((total, d), BF16),
+            pltpu.VMEM((total, d), BF16),
             pltpu.VMEM((ns, nb, 2 * rows, d // 2), BF16),
             pltpu.VMEM((ns, nb, 1, LANES), jnp.int32),
             pltpu.VMEM((nb, 2 * rows, d // 2), BF16),
@@ -502,21 +540,20 @@
         hold(w_out),
     )
     caption_grad, token_grad = pl.pallas_call(
-        functools.partial(token_kernel, patches),
+        write_kernel,
         out_shape=(
             jax.ShapeDtypeStruct((rows, d), F32),
             jax.ShapeDtypeStruct((total, d), F32),
         ),
-        in_specs=[vmem] * 5,
+        in_specs=[vmem, vmem],
         out_specs=(hbm, hbm),
         scratch_shapes=[
             pltpu.VMEM((rows, d), F32),
-            pltpu.VMEM((total, d), F32),
-            dma((d // GROUP + 1,)),
+            dma((2 * images + 1,)),
         ],
         compiler_params=pltpu.CompilerParams(vmem_limit_bytes=16 * 2**20),
-        name="token_grad",
-    )(summed, gk, gv, wk, wv)
+        name="write",
+    )(summed, token_terms)
     return (caption_grad, token_grad.reshape(images, patches, d))
 
 

time: 22 us -> 21.4 us (0.973)
  Pallas kernels: 21.2 us -> 20.5 us
    pallas_call x1, Pallas kernels: 1.73 us -> 1.01 us  [on_device(): pl.pallas_call(write_kernel, out_shape=(jax.ShapeDtypeStruct((rows, d), F...]
where the time goes in v5:
time: 21.4 us; the launch traced here: 21.2 us
  Pallas kernels  20.5 us (96%)
  between operations  0.64 us (3%)
    pallas_call x1, Pallas kernels, on_device(): pl.pallas_call(functools.partial(pair_kernel, nb, ns, images), out_shape=...  19.5 us
    pallas_call x1, Pallas kernels, on_device(): pl.pallas_call(write_kernel, out_shape=(jax.ShapeDtypeStruct((rows, d), F...  1.01 us

profile of v5, /device:TPU:0, one launch (start us, length us, event | category | flops | bytes accessed | tf_op | source)
XLA Modules:
  0.0 21.2 jit_solution(9315868471224171121)
XLA Ops:
  0.6 19.5 %pairs.1 = (f32[512,512]{1,0:T(8,128)S(1)}, f32[16,256]{1,0:T(8,128)S(1)}) custom-call(bf16[8,512]{1,0:T(8,128)(2,1)} %captions_hbm.1, s32[1,8]{1,0:T(1,128)} %bitcast.4, bf16[512,512]{1,0:T(8,128)(2,1)} %bitcast.3, bf16[512,512]{1,0:T(8,128)(2,1)} %wq_hbm.1, bf16[512,512]{1,0:T(8,128)(2,1)} %wk_hbm.1, bf16[512,512]{1,0:T(8,128)(2,1)} %wv_hbm.1, ...), custom_call_target="tpu_custom_call" | custom-call | tf_op jit(solution)/shard_map/pairs/pallas_call | solution.py:488
  20.2 1.0 %write.1 = (f32[8,512]{1,0:T(8,128)}, f32[512,512]{1,0:T(8,128)}) custom-call(f32[16,256]{1,0:T(8,128)S(1)} %get-tuple-element.6.sum_ref, f32[512,512]{1,0:T(8,128)S(1)} %get-tuple-element.7.token_ref), custom_call_target="tpu_custom_call" | custom-call | tf_op jit(solution)/shard_map/write/pallas_call | solution.py:542

commit v6 on v5

--- a/solution.py
+++ b/solution.py
@@ -234,14 +234,12 @@
 
     for load in loads[2:5]:
         load.wait()
-    for i in range(images):
-        at = pl.ds(i * patches, patches)
-        found = dot(tokens[at, :], wk[...])
-        keys[at, :] = found.astype(BF16)
-        keys_t[:, at] = found.astype(BF16).T
-        found = dot(tokens[at, :], wv[...])
-        values[at, :] = found.astype(BF16)
-        values_t[:, at] = found.astype(BF16).T
+    found = dot(tokens[...], wk[...]).astype(BF16)
+    keys[...] = found
+    keys_t[...] = found.T
+    found = dot(tokens[...], wv[...]).astype(BF16)
+    values[...] = found
+    values_t[...] = found.T
     if blocks > 1:
         gk[...] = jnp.zeros_like(gk)
         gv[...] = jnp.zeros_like(gv)
@@ -288,7 +286,7 @@
         query = (dot(caption.astype(BF16), wq[...]) * HEAD_DIM**-0.5).astype(BF16)
         queries = [head_stack(query[:, g * GROUP : (g + 1) * GROUP]) for g in range(groups)]
 
-        units = [(i, g) for i in range(images) for g in range(groups)]
+        units = [(i, g) for g in range(groups) for i in range(images)]
 
         def places(i, g):
             return (
@@ -297,20 +295,19 @@
                 slice(g * stacked, (g + 1) * stacked),
             )
 
-        def score(i, g):
-            at, cols, _ = places(i, g)
-            return dot_t(keys[at, cols], queries[g])
+        def score(g):
+            return dot_t(keys[:, g * GROUP : (g + 1) * GROUP], queries[g])
 
         pooled = [[] for _ in range(images)]
         inverse = [[] for _ in range(images)]
-        ahead = score(*units[0])
+        both = score(0)
         for n, (i, g) in enumerate(units):
             at, cols, to = places(i, g)
-            scores = ahead
-            if n + 1 < len(units):
-                ahead = score(*units[n + 1])
-            if n < len(before):
-                before[n]()
+            scores = both[at]
+            if i + 1 == images and g + 1 < groups:
+                both = score(g + 1)
+            for work in before[n :: len(units)]:
+                work()
             scores = jnp.exp(scores - jnp.max(scores, axis=0, keepdims=True))
             inverse[i].append(1.0 / jnp.sum(scores, axis=0, keepdims=True))
             weights = scores.astype(BF16)
@@ -372,6 +369,7 @@
             return grads, dot_t(values[at, cols], grads)
 
         grad_query = [None] * groups
+        stacked_scores = [[] for _ in range(groups)]
         ahead = grad_weight(*units[0])
         for n, (i, g) in enumerate(units):
             at, cols, to = places(i, g)
@@ -380,16 +378,32 @@
                 ahead = grad_weight(*units[n + 1])
             weights = weights_ref[which, at, to].astype(F32)
             grad_scores = (weights * (grad_weights - means[i][g])).astype(BF16)
-            later.append(
-                functools.partial(finish, at, cols, to, grads, grad_scores, queries[g], which)
-            )
+            stacked_scores[g].append(grad_scores)
+            works = [
+                functools.partial(
+                    finish, gv, gv_b, at, cols, weights_ref.at[which, at, to], grads, which
+                )
+            ]
+            if i + 1 == images:
+                works.append(
+                    functools.partial(
+                        finish,
+                        gk,
+                        gk_b,
+                        slice(0, images * patches),
+                        cols,
+                        jnp.concatenate(stacked_scores[g], axis=0),
+                        queries[g],
+                        which,
+                    )
+                )
             if own:
+                later.extend(works)
                 found = head_blocks(dot(keys_t[cols, at], grad_scores), block)
                 grad_query[g] = found if grad_query[g] is None else grad_query[g] + found
             else:
-                later.pop()()
-                if blocks == 1 and which == ns - 1 and g == groups - 1:
-                    token_product(at)
+                for work in works:
+                    work()
         if own:
             grad_query = jnp.concatenate(grad_query, axis=0).T * HEAD_DIM**-0.5
             grad = direct + dot_t(grad_query.astype(BF16), wq[...])
@@ -399,12 +413,8 @@
             ).astype(BF16)
         return later
 
-    def token_product(at):
-        token_out[at, :] = patches * (dot_t(gk_b[at, :], wk[...]) + dot_t(gv_b[at, :], wv[...]))
-
-    def finish(at, cols, to, grads, grad_scores, queries, which):
-        add(gv, gv_b, at, cols, dot(weights_ref[which, at, to], grads), which)
-        add(gk, gk_b, at, cols, dot(grad_scores, queries), which)
+    def finish(total, out, at, cols, left, right, which):
+        add(total, out, at, cols, dot(left[...], right), which)
 
     def run_all(which, own, before=()):
         if blocks == 1:
@@ -432,9 +442,7 @@
     if blocks > 1:
         gk_b[...] = gk[...].astype(BF16)
         gv_b[...] = gv[...].astype(BF16)
-    if blocks > 1 or ns == 1:
-        for i in range(images):
-            token_product(slice(i * patches, (i + 1) * patches))
+    token_out[...] = patches * (dot_t(gk_b[...], wk[...]) + dot_t(gv_b[...], wv[...]))
 
     all_parts.wait_recv()
 

time: 21.4 us -> 21.7 us (1.014)
  Pallas kernels: 20.5 us -> 20.8 us
    pallas_call x1, Pallas kernels: 19.5 us -> 19.8 us  [on_device(): pl.pallas_call(functools.partial(pair_kernel, nb, ns, images), out_shape=...]
where the time goes in v6:
time: 21.7 us; the launch traced here: 21.4 us
  Pallas kernels  20.8 us (96%)
  between operations  0.64 us (3%)
    pallas_call x1, Pallas kernels, on_device(): pl.pallas_call(functools.partial(pair_kernel, nb, ns, images), out_shape=...  19.8 us
    pallas_call x1, Pallas kernels, on_device(): pl.pallas_call(write_kernel, out_shape=(jax.ShapeDtypeStruct((rows, d), F...  1.01 us

profile of v6, /device:TPU:0, one launch (start us, length us, event | category | flops | bytes accessed | tf_op | source)
XLA Modules:
  0.0 21.4 jit_solution(3364631174709123259)
XLA Ops:
  0.6 19.8 %pairs.1 = (f32[512,512]{1,0:T(8,128)S(1)}, f32[16,256]{1,0:T(8,128)S(1)}) custom-call(bf16[8,512]{1,0:T(8,128)(2,1)} %captions_hbm.1, s32[1,8]{1,0:T(1,128)} %bitcast.4, bf16[512,512]{1,0:T(8,128)(2,1)} %bitcast.3, bf16[512,512]{1,0:T(8,128)(2,1)} %wq_hbm.1, bf16[512,512]{1,0:T(8,128)(2,1)} %wk_hbm.1, bf16[512,512]{1,0:T(8,128)(2,1)} %wv_hbm.1, ...), custom_call_target="tpu_custom_call" | custom-call | tf_op jit(solution)/shard_map/pairs/pallas_call | solution.py:496
  20.4 1.0 %write.1 = (f32[8,512]{1,0:T(8,128)}, f32[512,512]{1,0:T(8,128)}) custom-call(f32[16,256]{1,0:T(8,128)S(1)} %get-tuple-element.6.sum_ref, f32[512,512]{1,0:T(8,128)S(1)} %get-tuple-element.7.token_ref), custom_call_target="tpu_custom_call" | custom-call | tf_op jit(solution)/shard_map/write/pallas_call | solution.py:550

commit v7 on v5

--- a/solution.py
+++ b/solution.py
@@ -92,6 +92,7 @@
     cap_recv,
     owner_send,
     owner_recv,
+    sibling_sems,
     span_send,
     span_recv,
     span_owner_send,
@@ -112,8 +113,23 @@
     stacked = HEADS_IN_GROUP * block
     unroll = nb <= 16
 
+    cores = math.gcd(nb, 2)
+    chips = nb // cores
+    core = lax.rem(me, cores)
+    chip = me // cores
+    my_slot = core * chips + chip
+
     def peer_of(step):
         return lax.rem(me + step, nb)
+
+    def slot_of(device):
+        return lax.rem(device, cores) * chips + device // cores
+
+    def twin_of(step):
+        return lax.rem(chip + step, chips) * cores + core
+
+    def sibling_of(step):
+        return chip * cores + lax.rem(core + step, cores)
 
     def span_of(step):
         return lax.rem(my_span + step, ns)
@@ -153,8 +169,8 @@
     for load in loads[:2]:
         load.wait()
     mine = captions_ref[...].astype(F32)
-    caps[0, me] = jnp.concatenate([mine[:, :half], mine[:, half:]], axis=0).astype(BF16)
-    owners[0, me] = jnp.concatenate(
+    caps[0, my_slot] = jnp.concatenate([mine[:, :half], mine[:, half:]], axis=0).astype(BF16)
+    owners[0, my_slot] = jnp.concatenate(
         [owner_ref[...], jnp.zeros((1, LANES - rows), jnp.int32)], axis=1
     )
 
@@ -162,28 +178,28 @@
 
     def cap_copy(step):
         return pltpu.make_async_remote_copy(
-            src_ref=caps.at[0, me],
-            dst_ref=caps.at[0, me],
+            src_ref=caps.at[0, my_slot],
+            dst_ref=caps.at[0, my_slot],
             send_sem=cap_send,
             recv_sem=cap_recv,
-            device_id={"batch": peer_of(step)},
+            device_id={"batch": twin_of(step)},
             device_id_type=MESH,
         )
 
     def owner_copy(step):
         return pltpu.make_async_remote_copy(
-            src_ref=owners.at[0, me],
-            dst_ref=owners.at[0, me],
+            src_ref=owners.at[0, my_slot],
+            dst_ref=owners.at[0, my_slot],
             send_sem=owner_send,
             recv_sem=owner_recv,
-            device_id={"batch": peer_of(step)},
+            device_id={"batch": twin_of(step)},
             device_id_type=MESH,
         )
 
     def part_copy(step):
         return pltpu.make_async_remote_copy(
-            src_ref=part.at[peer_of(step)],
-            dst_ref=parts_in.at[me],
+            src_ref=part.at[slot_of(peer_of(step))],
+            dst_ref=parts_in.at[my_slot],
             send_sem=part_send,
             recv_sem=part_recv,
             device_id={"batch": peer_of(step)},
@@ -200,19 +216,30 @@
             device_id_type=MESH,
         )
 
-    def whole(ref, send_sem, recv_sem):
+    def whole(ref, count, send_sem, recv_sem):
         return pltpu.make_async_remote_copy(
-            src_ref=ref.at[pl.ds(0, nb - 1)],
-            dst_ref=ref.at[pl.ds(0, nb - 1)],
+            src_ref=ref.at[pl.ds(0, count)],
+            dst_ref=ref.at[pl.ds(0, count)],
             send_sem=send_sem,
             recv_sem=recv_sem,
             device_id={"batch": peer_of(1)},
             device_id_type=MESH,
         )
 
-    all_caps = whole(caps.at[0], cap_send, cap_recv)
-    all_owners = whole(owners.at[0], owner_send, owner_recv)
-    all_parts = whole(parts_in, part_send, part_recv)
+    all_caps = whole(caps.at[0], chips - 1, cap_send, cap_recv)
+    all_owners = whole(owners.at[0], chips - 1, owner_send, owner_recv)
+    all_parts = whole(parts_in, nb - 1, part_send, part_recv)
+
+    def sibling_copy(ref, step, sems, kind):
+        ours = ref.at[0, pl.ds(core * chips, chips)]
+        return pltpu.make_async_remote_copy(
+            src_ref=ours,
+            dst_ref=ours,
+            send_sem=sems.at[0, kind, step],
+            recv_sem=sems.at[1, kind, step],
+            device_id={"batch": sibling_of(step)},
+            device_id_type=MESH,
+        )
 
     def span_owner_copy(step, slot):
         return pltpu.make_async_remote_copy(
@@ -224,11 +251,11 @@
             device_id_type=MESH,
         )
 
-    @pl.loop(1, nb, unroll=unroll)
+    @pl.loop(1, chips, unroll=unroll)
     def _(step):
         cap_copy(step).start()
 
-    @pl.loop(1, nb, unroll=unroll)
+    @pl.loop(1, chips, unroll=unroll)
     def _(step):
         owner_copy(step).start()
 
@@ -248,12 +275,21 @@
     for load in loads[5:]:
         load.wait()
 
+    siblings = [
+        [sibling_copy(ref, step, sibling_sems, kind) for step in range(1, cores)]
+        for kind, ref in enumerate((caps, owners))
+    ]
     all_caps.wait_recv()
+    for copy in siblings[0]:
+        copy.start()
+    all_owners.wait_recv()
+    for copy in siblings[1]:
+        copy.start()
+    for copy in siblings[0] + siblings[1]:
+        copy.wait_recv()
 
     for step in range(1, ns):
         span_copy(step, ns - step).start()
-
-    all_owners.wait_recv()
 
     for step in range(1, ns):
         span_owner_copy(step, ns - step).start()
@@ -438,10 +474,12 @@
 
     all_parts.wait_recv()
 
-    parts_in[me] = part[me]
+    parts_in[my_slot] = part[my_slot]
     sum_out[...] = jnp.sum(parts_in[...].astype(F32), axis=0)
 
     all_caps.wait_send()
+    for copy in siblings[0] + siblings[1]:
+        copy.wait_send()
     all_owners.wait_send()
     all_parts.wait_send()
 
@@ -519,6 +557,7 @@
             dma,
             dma,
             dma,
+            dma((2, 2, 2)),
             dma((ns,)),
             dma((ns,)),
             dma((ns,)),

time: 21.4 us -> 21.9 us (1.023)
  Pallas kernels: 20.5 us -> 21 us
    pallas_call x1, Pallas kernels: 19.5 us -> 20 us  [on_device(): pl.pallas_call(functools.partial(pair_kernel, nb, ns, images), out_shape=...]
where the time goes in v7:
time: 21.9 us; the launch traced here: 21.7 us
  Pallas kernels  21 us (96%)
  between operations  0.64 us (3%)
    pallas_call x1, Pallas kernels, on_device(): pl.pallas_call(functools.partial(pair_kernel, nb, ns, images), out_shape=...  20 us
    pallas_call x1, Pallas kernels, on_device(): pl.pallas_call(write_kernel, out_shape=(jax.ShapeDtypeStruct((rows, d), F...  1.01 us

profile of v7, /device:TPU:0, one launch (start us, length us, event | category | flops | bytes accessed | tf_op | source)
XLA Modules:
  0.0 21.7 jit_solution(5976871688494028553)
XLA Ops:
  0.6 20.0 %pairs.1 = (f32[512,512]{1,0:T(8,128)S(1)}, f32[16,256]{1,0:T(8,128)S(1)}) custom-call(bf16[8,512]{1,0:T(8,128)(2,1)} %captions_hbm.1, s32[1,8]{1,0:T(1,128)} %bitcast.4, bf16[512,512]{1,0:T(8,128)(2,1)} %bitcast.3, bf16[512,512]{1,0:T(8,128)(2,1)} %wq_hbm.1, bf16[512,512]{1,0:T(8,128)(2,1)} %wk_hbm.1, bf16[512,512]{1,0:T(8,128)(2,1)} %wv_hbm.1, ...), custom_call_target="tpu_custom_call" | custom-call | tf_op jit(solution)/shard_map/pairs/pallas_call | solution.py:526
  20.7 1.0 %write.1 = (f32[8,512]{1,0:T(8,128)}, f32[512,512]{1,0:T(8,128)}) custom-call(f32[16,256]{1,0:T(8,128)S(1)} %get-tuple-element.6.sum_ref, f32[512,512]{1,0:T(8,128)S(1)} %get-tuple-element.7.token_ref), custom_call_target="tpu_custom_call" | custom-call | tf_op jit(solution)/shard_map/write/pallas_call | solution.py:581

commit v8 on v5

--- a/solution.py
+++ b/solution.py
@@ -228,20 +228,20 @@
     def _(step):
         cap_copy(step).start()
 
-    @pl.loop(1, nb, unroll=unroll)
-    def _(step):
-        owner_copy(step).start()
-
     for load in loads[2:5]:
         load.wait()
     for i in range(images):
         at = pl.ds(i * patches, patches)
         found = dot(tokens[at, :], wk[...])
         keys[at, :] = found.astype(BF16)
-        keys_t[:, at] = found.astype(BF16).T
         found = dot(tokens[at, :], wv[...])
         values[at, :] = found.astype(BF16)
         values_t[:, at] = found.astype(BF16).T
+
+    @pl.loop(1, nb, unroll=unroll)
+    def _(step):
+        owner_copy(step).start()
+
     if blocks > 1:
         gk[...] = jnp.zeros_like(gk)
         gv[...] = jnp.zeros_like(gv)
@@ -253,10 +253,14 @@
     for step in range(1, ns):
         span_copy(step, ns - step).start()
 
-    all_owners.wait_recv()
-
-    for step in range(1, ns):
-        span_owner_copy(step, ns - step).start()
+    def turn_keys(i):
+        at = slice(i * patches, (i + 1) * patches)
+        keys_t[:, at] = keys[at, :].T
+
+    def pass_owners():
+        all_owners.wait_recv()
+        for step in range(1, ns):
+            span_owner_copy(step, ns - step).start()
 
     def add(total, out, at, cols, found, which):
         if blocks > 1 or which > 0:
@@ -266,7 +270,7 @@
         else:
             total[at, cols] = found
 
-    def run_block(slot, which, own, before=()):
+    def run_block(slot, which, own, before=(), arrive=None):
         later = []
         held = caps[which, pl.ds(slot, slots)].astype(F32)
         caption = jnp.concatenate(
@@ -275,15 +279,6 @@
                 held[:, rows:].reshape(block, half),
             ],
             axis=1,
-        )
-        owner = owners[which, pl.ds(slot, slots)]
-        owner = jnp.broadcast_to(owner, (slots, rows, LANES))
-        row = lax.broadcasted_iota(jnp.int32, owner.shape, 1)
-        lane = lax.broadcasted_iota(jnp.int32, owner.shape, 2)
-        owner = jnp.sum(
-            jnp.where(row == lane, owner, 0).astype(F32).reshape(block, LANES),
-            axis=1,
-            keepdims=True,
         )
         query = (dot(caption.astype(BF16), wq[...]) * HEAD_DIM**-0.5).astype(BF16)
         queries = [head_stack(query[:, g * GROUP : (g + 1) * GROUP]) for g in range(groups)]
@@ -318,6 +313,17 @@
             pooled[i].append(head_blocks(dot(values_t[cols, at], weights) * inverse[i][g], block))
         pooled_t = pooled
         pooled = [jnp.concatenate(found, axis=0).T.astype(BF16) for found in pooled]
+        if arrive is not None:
+            arrive()
+        owner = owners[which, pl.ds(slot, slots)]
+        owner = jnp.broadcast_to(owner, (slots, rows, LANES))
+        row = lax.broadcasted_iota(jnp.int32, owner.shape, 1)
+        lane = lax.broadcasted_iota(jnp.int32, owner.shape, 2)
+        owner = jnp.sum(
+            jnp.where(row == lane, owner, 0).astype(F32).reshape(block, LANES),
+            axis=1,
+            keepdims=True,
+        )
         mixed = dot(jnp.concatenate(pooled, axis=0), wo[...])
         caption_2 = jnp.concatenate([caption] * images, axis=0)
         owner_2 = jnp.concatenate([owner] * images, axis=0)
@@ -406,9 +412,14 @@
         add(gv, gv_b, at, cols, dot(weights_ref[which, at, to], grads), which)
         add(gk, gk_b, at, cols, dot(grad_scores, queries), which)
 
-    def run_all(which, own, before=()):
+    def run_all(which, own, before=(), arrive=None):
         if blocks == 1:
-            return run_block(0, which, own, before)
+            return run_block(0, which, own, before, arrive)
+
+        for work in before:
+            work()
+        if arrive is not None:
+            arrive()
 
         @pl.loop(0, blocks)
         def _(n):
@@ -417,7 +428,8 @@
 
         return []
 
-    later = run_all(0, True)
+    turns = [functools.partial(turn_keys, i) for i in range(images)]
+    later = run_all(0, True, turns, pass_owners)
 
     @pl.loop(1, nb, unroll=unroll)
     def _(step):

time: 21.4 us -> 21.4 us (level)
  no operation moved by 1% of the time
where the time goes in v8:
time: 21.4 us; the launch traced here: 21.2 us
  Pallas kernels  20.5 us (96%)
  between operations  0.64 us (3%)
    pallas_call x1, Pallas kernels, on_device(): pl.pallas_call(functools.partial(pair_kernel, nb, ns, images), out_shape=...  19.5 us
    pallas_call x1, Pallas kernels, on_device(): pl.pallas_call(write_kernel, out_shape=(jax.ShapeDtypeStruct((rows, d), F...  1.01 us

profile of v8, /device:TPU:0, one launch (start us, length us, event | category | flops | bytes accessed | tf_op | source)
XLA Modules:
  0.0 21.2 jit_solution(3750650181148831074)
XLA Ops:
  0.6 19.5 %pairs.1 = (f32[512,512]{1,0:T(8,128)S(1)}, f32[16,256]{1,0:T(8,128)S(1)}) custom-call(bf16[8,512]{1,0:T(8,128)(2,1)} %captions_hbm.1, s32[1,8]{1,0:T(1,128)} %bitcast.4, bf16[512,512]{1,0:T(8,128)(2,1)} %bitcast.3, bf16[512,512]{1,0:T(8,128)(2,1)} %wq_hbm.1, bf16[512,512]{1,0:T(8,128)(2,1)} %wk_hbm.1, bf16[512,512]{1,0:T(8,128)(2,1)} %wv_hbm.1, ...), custom_call_target="tpu_custom_call" | custom-call | tf_op jit(solution)/shard_map/pairs/pallas_call | solution.py:500
  20.2 1.0 %write.1 = (f32[8,512]{1,0:T(8,128)}, f32[512,512]{1,0:T(8,128)}) custom-call(f32[16,256]{1,0:T(8,128)S(1)} %get-tuple-element.6.sum_ref, f32[512,512]{1,0:T(8,128)S(1)} %get-tuple-element.7.token_ref), custom_call_target="tpu_custom_call" | custom-call | tf_op jit(solution)/shard_map/write/pallas_call | solution.py:554

commit v9 on v5

--- a/solution.py
+++ b/solution.py
@@ -311,9 +311,14 @@
                 ahead = score(*units[n + 1])
             if n < len(before):
                 before[n]()
-            scores = jnp.exp(scores - jnp.max(scores, axis=0, keepdims=True))
-            inverse[i].append(1.0 / jnp.sum(scores, axis=0, keepdims=True))
-            weights = scores.astype(BF16)
+            rows_ = []
+            weights = []
+            for part_ in by_head(scores, block):
+                part_ = jnp.exp(part_ - jnp.max(part_, axis=0, keepdims=True))
+                rows_.append(1.0 / jnp.sum(part_, axis=0, keepdims=True))
+                weights.append(part_.astype(BF16))
+            inverse[i].append(jnp.concatenate(rows_, axis=1))
+            weights = jnp.concatenate(weights, axis=1)
             weights_ref[which, at, to] = weights
             pooled[i].append(head_blocks(dot(values_t[cols, at], weights) * inverse[i][g], block))
         pooled_t = pooled

time: 21.4 us -> 21.4 us (level)
  no operation moved by 1% of the time
where the time goes in v9:
time: 21.4 us; the launch traced here: 21.2 us
  Pallas kernels  20.5 us (96%)
  between operations  0.64 us (3%)
    pallas_call x1, Pallas kernels, on_device(): pl.pallas_call(functools.partial(pair_kernel, nb, ns, images), out_shape=...  19.5 us
    pallas_call x1, Pallas kernels, on_device(): pl.pallas_call(write_kernel, out_shape=(jax.ShapeDtypeStruct((rows, d), F...  1.01 us

profile of v9, /device:TPU:0, one launch (start us, length us, event | category | flops | bytes accessed | tf_op | source)
XLA Modules:
  0.0 21.2 jit_solution(10596883893106945372)
XLA Ops:
  0.6 19.5 %pairs.1 = (f32[512,512]{1,0:T(8,128)S(1)}, f32[16,256]{1,0:T(8,128)S(1)}) custom-call(bf16[8,512]{1,0:T(8,128)(2,1)} %captions_hbm.1, s32[1,8]{1,0:T(1,128)} %bitcast.4, bf16[512,512]{1,0:T(8,128)(2,1)} %bitcast.3, bf16[512,512]{1,0:T(8,128)(2,1)} %wq_hbm.1, bf16[512,512]{1,0:T(8,128)(2,1)} %wk_hbm.1, bf16[512,512]{1,0:T(8,128)(2,1)} %wv_hbm.1, ...), custom_call_target="tpu_custom_call" | custom-call | tf_op jit(solution)/shard_map/pairs/pallas_call | solution.py:493
  20.1 1.0 %write.1 = (f32[8,512]{1,0:T(8,128)}, f32[512,512]{1,0:T(8,128)}) custom-call(f32[16,256]{1,0:T(8,128)S(1)} %get-tuple-element.6.sum_ref, f32[512,512]{1,0:T(8,128)S(1)} %get-tuple-element.7.token_ref), custom_call_target="tpu_custom_call" | custom-call | tf_op jit(solution)/shard_map/write/pallas_call | solution.py:547
